TPU v7x, 512 devices: a whole 4x8x8 slice. The times are simulated.
512 devices in a mesh: shot: 16 (over y, core), tile: 32 (over x, z).
Axes of the slice: x: 4, y: 8, z: 8, core: 2. Of those that a mesh axis runs over, the one named last changes fastest.
Arguments:
- tile_store: int32 [512], replicated, may hold values from 0 to 511, as said below
- apertures: int32 [512, 32], P(('shot', 'tile')), may hold values from 0 to 511, as said below
- model: bfloat16 [512, 2, 4096], P('tile'), may hold values from 0.3984375 to 1.296875
- fwd_states: float32 [512, 2, 64, 16, 128], P(('shot', 'tile')), may hold values from -0.6 to 0.6
- adj_states: float32 [512, 2, 64, 16, 128], P(('shot', 'tile')), may hold values from -0.6 to 0.6
- source_cell: int32 [512], P(('shot', 'tile')), may hold values from 0 to 131071
- wavelet: float32 [512, 8], P(('shot', 'tile')), may hold values from -6 to 6
- receiver_cells: int32 [512, 256], P(('shot', 'tile')), may hold values from 0 to 131071
- residuals: float32 [512, 8, 256], P(('shot', 'tile')), may hold values from -6 to 6
Outputs:
- gradient: float32 [512, 2, 4096], P('tile', None, 'shot')
Inputs may be any that keep to these rules, and one draw needn't show every extreme that they name: `tile_store`: A permutation of the tile numbers; the tile in row r of model is held by device r // 16 of tile. `apertures`: each row names 32 distinct tiles; at most 2 of them lie in rows of model held by one device of tile, and in every row some device holds exactly 2 of them.
All inputs are finite; a program needn't handle non-finite values.
Results may differ from a plain program's by a relative error of at most 0.0011.
Values may be sent and summed in bfloat16 or wider, within the bound.
A program may use at most 128 MiB of HBM per device.

v0:
```python
import jax
import jax.numpy as jnp
from jax import lax
from jax.sharding import PartitionSpec as P

B = 16
APX = 4
APZ = 8


COEF_SECOND = (-205.0 / 72.0, 8.0 / 5.0, -1.0 / 5.0, 8.0 / 315.0, -1.0 / 560.0)
COEF_FIRST = (4.0 / 5.0, -1.0 / 5.0, 4.0 / 105.0, -1.0 / 280.0)
SPEED_SCALE = 0.12


def neighbours(wave_field, which_axis):
    extent = wave_field.shape[which_axis]
    pad_spec = [(0, 0), (0, 0), (0, 0)]
    pad_spec[which_axis] = (4, 4)
    padded = jnp.pad(wave_field, pad_spec)
    return [
        lax.slice_in_dim(padded, 4 + offset, 4 + offset + extent, axis=which_axis)
        for offset in range(-4, 5)
    ]


def second_sum(wave_field):
    summed = 3.0 * COEF_SECOND[0] * wave_field
    for which_axis in range(3):
        shifts = neighbours(wave_field, which_axis)
        for reach in range(1, 5):
            summed = summed + COEF_SECOND[reach] * (shifts[4 + reach] + shifts[4 - reach])
    return summed


def first_along(wave_field, which_axis):
    shifts = neighbours(wave_field, which_axis)
    summed = COEF_FIRST[0] * (shifts[5] - shifts[3])
    for reach in range(2, 5):
        summed = summed + COEF_FIRST[reach - 1] * (shifts[4 + reach] - shifts[4 - reach])
    return summed


def operate(wave_field, gain_field, slopes):
    summed = gain_field * second_sum(wave_field)
    for which_axis in range(3):
        summed = summed + slopes[which_axis] * first_along(wave_field, which_axis)
    return summed


def to_volume(tile_block):
    blocks = tile_block.reshape(APX, APZ, 2, B, B, B)
    return blocks.transpose(2, 0, 3, 4, 1, 5).reshape(2, APX * B, B, APZ * B)


def to_tiles(volume):
    blocks = volume.reshape(2, APX, B, B, APZ, B).transpose(1, 4, 0, 2, 3, 5)
    return blocks.reshape(APX * APZ, 2, B * B * B)


def evolve(coeffs, fwd_pair, adj_pair, source_at, pulses, listen_at, traces):
    speed = SPEED_SCALE * coeffs[0]
    gain_field = coeffs[1]
    slopes = [first_along(gain_field, which_axis) for which_axis in range(3)]
    volume_shape = speed.shape

    def inject(wave_field, cells, amounts):
        return wave_field.reshape(-1).at[cells].add(amounts).reshape(volume_shape)

    def forward_step(carry, pulse):
        older, current = carry
        applied = operate(current, gain_field, slopes)
        newer = inject(
            2.0 * current - older + speed * applied, source_at.reshape(1), pulse.reshape(1)
        )
        return ((current, newer), (current, applied))

    unused, (states, images) = lax.scan(forward_step, (fwd_pair[0], fwd_pair[1]), pulses)

    def adjoint_step(carry, inputs):
        later, current, grad_speed, grad_gain = carry
        state, image, listened = inputs
        newer = inject(
            2.0 * current - later + speed * operate(current, gain_field, slopes),
            listen_at,
            listened,
        )
        grad_speed = grad_speed + newer * image
        product = first_along(newer, 0) * first_along(state, 0)
        product = product + first_along(newer, 1) * first_along(state, 1)
        product = product + first_along(newer, 2) * first_along(state, 2)
        grad_gain = grad_gain + speed * product
        return ((current, newer, grad_speed, grad_gain), None)

    zeros_field = jnp.zeros(volume_shape, jnp.float32)
    final_carry, unused_out = lax.scan(
        adjoint_step,
        (adj_pair[0], adj_pair[1], zeros_field, zeros_field),
        (states, images, traces),
        reverse=True,
    )
    return jnp.stack([final_carry[2], final_carry[3]])


def per_device(
    tile_store,
    apertures,
    model,
    fwd_states,
    adj_states,
    source_cell,
    wavelet,
    receiver_cells,
    residuals,
):
    owner_total = lax.axis_size("tile")
    per_owner = model.shape[0]
    tile_cells = model.shape[2]
    wanted = apertures[0]
    tile_count = wanted.shape[0]
    capacity = max(2, (2 * tile_count + owner_total - 1) // owner_total)
    store_rows = tile_store[wanted]
    owner_ids = store_rows // per_owner
    slot_ids = store_rows % per_owner
    position = jnp.arange(tile_count)
    before = (owner_ids[None, :] == owner_ids[:, None]) & (position[None, :] < position[:, None])
    slot_rank = jnp.sum(before.astype(jnp.int32), axis=1)
    placed_at = owner_ids * capacity + slot_rank
    slot_total = owner_total * capacity
    matches = placed_at[:, None] == jnp.arange(slot_total)[None, :]
    requests = jnp.sum(jnp.where(matches, slot_ids[:, None] + 1, 0), axis=0).reshape(
        owner_total, capacity
    )
    empty_tiles = jnp.zeros((tile_count, 2, tile_cells), jnp.bfloat16)
    shard_rows = lax.all_gather(model, "tile", axis=0, tiled=True)
    inside = (store_rows >= 0) & (store_rows < shard_rows.shape[0])
    chosen = shard_rows[jnp.clip(store_rows, 0, shard_rows.shape[0] - 1)]
    fetched_tiles = jnp.where(inside[:, None, None], chosen, empty_tiles)
    coeffs = to_volume(fetched_tiles.astype(jnp.float32))
    volume = evolve(
        coeffs,
        fwd_states[0],
        adj_states[0],
        source_cell[0],
        wavelet[0],
        receiver_cells[0],
        residuals[0],
    )
    shot_tiles = to_tiles(volume)
    outgoing = jnp.zeros((slot_total, 2, tile_cells), jnp.float32).at[placed_at].set(shot_tiles)
    outgoing = outgoing.reshape(owner_total, capacity, 2, tile_cells)
    incoming, arrived = (
        lax.all_to_all(outgoing, "tile", split_axis=0, concat_axis=0, tiled=True),
        lax.all_to_all(requests, "tile", split_axis=0, concat_axis=0, tiled=True),
    )
    select = (arrived.reshape(1, -1) == (jnp.arange(per_owner) + 1)[:, None]).astype(jnp.float32)
    owned_sum = jnp.dot(
        select,
        incoming.reshape(slot_total, 2 * tile_cells),
        precision=lax.Precision.HIGHEST,
        preferred_element_type=jnp.float32,
    )
    owned_sum = owned_sum.reshape(per_owner, 2, tile_cells)
    return lax.psum_scatter(owned_sum, "shot", scatter_dimension=2, tiled=True)


def solution(mesh):
    return jax.shard_map(
        per_device,
        mesh=mesh,
        in_specs=(
            P(),
            P(("shot", "tile"), None),
            P("tile", None, None),
            P(("shot", "tile"), None, None, None, None),
            P(("shot", "tile"), None, None, None, None),
            P(("shot", "tile")),
            P(("shot", "tile"), None),
            P(("shot", "tile"), None),
            P(("shot", "tile"), None, None),
        ),
        out_specs=P("tile", None, "shot"),
        check_vma=False,
    )
```

profile of v0, /device:TPU:1, one launch (start us, length us, event | category | flops | bytes accessed | tf_op | source)
XLA Modules:
  0.0 549.6 jit_solution(18261868613116901082)
XLA Ops:
  9.7 13.7 %all-to-all-start = ((s32[32,1,2]{2,1,0:T(1,128)}), s32[32,1,2]{2,1,0:T(1,128)S(1)}, u32[]{:S(2)}, u32[]{:S(2)}) async-start(s32[32,1,2]{2,1,0:T(1,128)} %bitcast.7), calls=%async_computation | async-start | bytes 32768 | tf_op jit(solution)/shard_map/all_to_all | solution.py:154
  24.2 2.1 slice_bitcast_fusion
  26.3 2.3 slice_bitcast_fusion.2
  28.6 91.6 %all-gather.2.cloned.1.call-done = bf16[512,2,4096]{2,1,0:T(2,128)(2,1)} async-done(((bf16[16,2,4096]{2,1,0:T(2,128)(2,1)}), bf16[512,2,4096]{2,1,0:T(2,128)(2,1)}) %all-gather.2.cloned.1.call-update) | async-done | bytes 8388624 | tf_op jit(solution)/shard_map/all_gather | solution.py:135
  120.2 5.0 gather_fusion.1
  125.2 4.1 gather.13
  129.3 2.8 convert_bitcast_fusion
  132.1 2.7 slice_multiply_fusion
  134.8 4.4 copy.32
  139.2 3.2 squeeze.64
  144.2 6.6 %copy.33 = f32[1,4,16,16,8,16]{5,4,3,2,1,0:T(8,128)} copy(f32[1,4,16,16,8,16]{5,3,2,0,4,1:T(8,128)} %get-tuple-element.562) | data formatting | bytes 1048576 | tf_op jit(solution)/shard_map/mul | solution.py:62
  150.8 3.3 mul.809
  154.0 32.5 %while.40 = (s32[]{:T(128)}, f32[64,16,128]{2,1,0:T(8,128)}, f32[64,16,128]{2,1,0:T(8,128)S(1)}, f32[8,64,16,128]{3,2,1,0:T(8,128)}, f32[8,64,16,128]{3,2,1,0:T(...) while((s32[]{:T(128)}, f32[64,16,128]{2,1,0:T(8,128)}, ...), condition=%wide.region_3.4_spmd, body=%wide.region_2.3_spmd.sunk | while | flops 10616836 | bytes 11012266 | solution.py:78
  154.2 2.9 bitcast_dynamic-update-slice_fusion.3
  158.3 2.8 bitcast_dynamic-update-slice_fusion.3
  162.3 2.8 bitcast_dynamic-update-slice_fusion.3
  166.4 2.8 bitcast_dynamic-update-slice_fusion.3
  170.4 2.8 bitcast_dynamic-update-slice_fusion.3
  174.4 2.8 bitcast_dynamic-update-slice_fusion.3
  178.5 2.9 bitcast_dynamic-update-slice_fusion.3
  182.5 2.9 bitcast_dynamic-update-slice_fusion.3
  186.6 207.4 %while.41 = (s32[]{:T(128)}, f32[64,16,128]{2,1,0:T(8,128)}, f32[64,16,128]{2,1,0:T(8,128)}, f32[64,16,128]{2,1,0:T(8,128)}, f32[64,16,128]{2,1,0:T(8,128)}, /*i...) while((s32[]{:T(128)}, f32[64,16,128]{2,1,0:T(8,128)}, ...), condition=%wide.region_6.7_spmd.clone, body=%wide.region_4.6_spmd.clone.sunk | while | flops 20710404 | bytes 13639899 | solution.py:96
  186.6 8.8 %multiply_add_fusion.8 = f32[64,16,128]{2,1,0:T(8,128)S(1)} fusion(f32[64,16,128]{2,1,0:T(8,128)S(1)} %get-tuple-element.834, f32[64,16,128]{2,1,0:T(8,128)S(1)} %get-tuple-element.833, f32[64,16,128]{2,1,0:T(8,128)S(1)} %get-tuple-element.832, f32[64,16,128]{2,1,0:T(8,128)S(1)} %get-tuple-element.831, f32[64,16,128]{2,1,0:T(8,128)S(1)} %get-tuple-element.830, ...), kind=kLoop, calls=%fused_computation.182.clone.1 | loop fusion | flops 10616832 | bytes 4194304 | tf_op jit(solution)/shard_map/while/body/eval_jaxpr/add | solution.py:84
  196.1 2.2 scatter_fusion
  198.3 1.9 dynamic-slice_bitcast_fusion.2
  200.1 10.5 %fusion.123 = (f32[64,16,128]{2,1,0:T(8,128)}, f32[64,16,128]{2,1,0:T(8,128)}) fusion(f32[64,16,128]{2,1,0:T(8,128)S(1)} %get-tuple-element.834, f32[64,16,128]{2,1,0:T(8,128)S(1)} %bitcast.104, f32[64,16,128]{2,1,0:T(8,128)} %dynamic-slice_bitcast_fusion.2, f32[64,16,128]{2,1,0:T(8,128)} %get-tuple-element.812, pred[]{:T(512)S(6)} %compare.60, ...), kind=kLoop, calls=%fused_computation.115.clone.1 | loop fusion | flops 10092544 | bytes 4194309 | tf_op jit(solution)/shard_map/while/body/eval_jaxpr/add | solution.py:92
  212.3 8.8 %multiply_add_fusion.8 = f32[64,16,128]{2,1,0:T(8,128)S(1)} fusion(f32[64,16,128]{2,1,0:T(8,128)S(1)} %get-tuple-element.834, f32[64,16,128]{2,1,0:T(8,128)S(1)} %get-tuple-element.833, f32[64,16,128]{2,1,0:T(8,128)S(1)} %get-tuple-element.832, f32[64,16,128]{2,1,0:T(8,128)S(1)} %get-tuple-element.831, f32[64,16,128]{2,1,0:T(8,128)S(1)} %get-tuple-element.830, ...), kind=kLoop, calls=%fused_computation.182.clone.1 | loop fusion | flops 10616832 | bytes 4194304 | tf_op jit(solution)/shard_map/while/body/eval_jaxpr/add | solution.py:84
  221.8 2.2 scatter_fusion
  224.0 1.9 dynamic-slice_bitcast_fusion.2
  225.8 10.8 %fusion.123 = (f32[64,16,128]{2,1,0:T(8,128)}, f32[64,16,128]{2,1,0:T(8,128)}) fusion(f32[64,16,128]{2,1,0:T(8,128)S(1)} %get-tuple-element.834, f32[64,16,128]{2,1,0:T(8,128)S(1)} %bitcast.104, f32[64,16,128]{2,1,0:T(8,128)} %dynamic-slice_bitcast_fusion.2, f32[64,16,128]{2,1,0:T(8,128)} %get-tuple-element.812, pred[]{:T(512)S(6)} %compare.60, ...), kind=kLoop, calls=%fused_computation.115.clone.1 | loop fusion | flops 10092544 | bytes 4194309 | tf_op jit(solution)/shard_map/while/body/eval_jaxpr/add | solution.py:92
  238.3 8.8 %multiply_add_fusion.8 = f32[64,16,128]{2,1,0:T(8,128)S(1)} fusion(f32[64,16,128]{2,1,0:T(8,128)S(1)} %get-tuple-element.834, f32[64,16,128]{2,1,0:T(8,128)S(1)} %get-tuple-element.833, f32[64,16,128]{2,1,0:T(8,128)S(1)} %get-tuple-element.832, f32[64,16,128]{2,1,0:T(8,128)S(1)} %get-tuple-element.831, f32[64,16,128]{2,1,0:T(8,128)S(1)} %get-tuple-element.830, ...), kind=kLoop, calls=%fused_computation.182.clone.1 | loop fusion | flops 10616832 | bytes 4194304 | tf_op jit(solution)/shard_map/while/body/eval_jaxpr/add | solution.py:84
  247.8 2.2 scatter_fusion
  249.9 1.9 dynamic-slice_bitcast_fusion.2
  251.8 10.8 %fusion.123 = (f32[64,16,128]{2,1,0:T(8,128)}, f32[64,16,128]{2,1,0:T(8,128)}) fusion(f32[64,16,128]{2,1,0:T(8,128)S(1)} %get-tuple-element.834, f32[64,16,128]{2,1,0:T(8,128)S(1)} %bitcast.104, f32[64,16,128]{2,1,0:T(8,128)} %dynamic-slice_bitcast_fusion.2, f32[64,16,128]{2,1,0:T(8,128)} %get-tuple-element.812, pred[]{:T(512)S(6)} %compare.60, ...), kind=kLoop, calls=%fused_computation.115.clone.1 | loop fusion | flops 10092544 | bytes 4194309 | tf_op jit(solution)/shard_map/while/body/eval_jaxpr/add | solution.py:92
  264.2 8.8 %multiply_add_fusion.8 = f32[64,16,128]{2,1,0:T(8,128)S(1)} fusion(f32[64,16,128]{2,1,0:T(8,128)S(1)} %get-tuple-element.834, f32[64,16,128]{2,1,0:T(8,128)S(1)} %get-tuple-element.833, f32[64,16,128]{2,1,0:T(8,128)S(1)} %get-tuple-element.832, f32[64,16,128]{2,1,0:T(8,128)S(1)} %get-tuple-element.831, f32[64,16,128]{2,1,0:T(8,128)S(1)} %get-tuple-element.830, ...), kind=kLoop, calls=%fused_computation.182.clone.1 | loop fusion | flops 10616832 | bytes 4194304 | tf_op jit(solution)/shard_map/while/body/eval_jaxpr/add | solution.py:84
  273.7 2.2 scatter_fusion
  275.9 1.9 dynamic-slice_bitcast_fusion.2
  277.8 10.8 %fusion.123 = (f32[64,16,128]{2,1,0:T(8,128)}, f32[64,16,128]{2,1,0:T(8,128)}) fusion(f32[64,16,128]{2,1,0:T(8,128)S(1)} %get-tuple-element.834, f32[64,16,128]{2,1,0:T(8,128)S(1)} %bitcast.104, f32[64,16,128]{2,1,0:T(8,128)} %dynamic-slice_bitcast_fusion.2, f32[64,16,128]{2,1,0:T(8,128)} %get-tuple-element.812, pred[]{:T(512)S(6)} %compare.60, ...), kind=kLoop, calls=%fused_computation.115.clone.1 | loop fusion | flops 10092544 | bytes 4194309 | tf_op jit(solution)/shard_map/while/body/eval_jaxpr/add | solution.py:92
  290.2 8.8 %multiply_add_fusion.8 = f32[64,16,128]{2,1,0:T(8,128)S(1)} fusion(f32[64,16,128]{2,1,0:T(8,128)S(1)} %get-tuple-element.834, f32[64,16,128]{2,1,0:T(8,128)S(1)} %get-tuple-element.833, f32[64,16,128]{2,1,0:T(8,128)S(1)} %get-tuple-element.832, f32[64,16,128]{2,1,0:T(8,128)S(1)} %get-tuple-element.831, f32[64,16,128]{2,1,0:T(8,128)S(1)} %get-tuple-element.830, ...), kind=kLoop, calls=%fused_computation.182.clone.1 | loop fusion | flops 10616832 | bytes 4194304 | tf_op jit(solution)/shard_map/while/body/eval_jaxpr/add | solution.py:84
  299.7 2.2 scatter_fusion
  301.8 1.9 dynamic-slice_bitcast_fusion.2
  303.7 10.8 %fusion.123 = (f32[64,16,128]{2,1,0:T(8,128)}, f32[64,16,128]{2,1,0:T(8,128)}) fusion(f32[64,16,128]{2,1,0:T(8,128)S(1)} %get-tuple-element.834, f32[64,16,128]{2,1,0:T(8,128)S(1)} %bitcast.104, f32[64,16,128]{2,1,0:T(8,128)} %dynamic-slice_bitcast_fusion.2, f32[64,16,128]{2,1,0:T(8,128)} %get-tuple-element.812, pred[]{:T(512)S(6)} %compare.60, ...), kind=kLoop, calls=%fused_computation.115.clone.1 | loop fusion | flops 10092544 | bytes 4194309 | tf_op jit(solution)/shard_map/while/body/eval_jaxpr/add | solution.py:92
  316.1 8.8 %multiply_add_fusion.8 = f32[64,16,128]{2,1,0:T(8,128)S(1)} fusion(f32[64,16,128]{2,1,0:T(8,128)S(1)} %get-tuple-element.834, f32[64,16,128]{2,1,0:T(8,128)S(1)} %get-tuple-element.833, f32[64,16,128]{2,1,0:T(8,128)S(1)} %get-tuple-element.832, f32[64,16,128]{2,1,0:T(8,128)S(1)} %get-tuple-element.831, f32[64,16,128]{2,1,0:T(8,128)S(1)} %get-tuple-element.830, ...), kind=kLoop, calls=%fused_computation.182.clone.1 | loop fusion | flops 10616832 | bytes 4194304 | tf_op jit(solution)/shard_map/while/body/eval_jaxpr/add | solution.py:84
  325.6 2.2 scatter_fusion
  327.8 1.9 dynamic-slice_bitcast_fusion.2
  329.7 10.8 %fusion.123 = (f32[64,16,128]{2,1,0:T(8,128)}, f32[64,16,128]{2,1,0:T(8,128)}) fusion(f32[64,16,128]{2,1,0:T(8,128)S(1)} %get-tuple-element.834, f32[64,16,128]{2,1,0:T(8,128)S(1)} %bitcast.104, f32[64,16,128]{2,1,0:T(8,128)} %dynamic-slice_bitcast_fusion.2, f32[64,16,128]{2,1,0:T(8,128)} %get-tuple-element.812, pred[]{:T(512)S(6)} %compare.60, ...), kind=kLoop, calls=%fused_computation.115.clone.1 | loop fusion | flops 10092544 | bytes 4194309 | tf_op jit(solution)/shard_map/while/body/eval_jaxpr/add | solution.py:92
  342.1 8.8 %multiply_add_fusion.8 = f32[64,16,128]{2,1,0:T(8,128)S(1)} fusion(f32[64,16,128]{2,1,0:T(8,128)S(1)} %get-tuple-element.834, f32[64,16,128]{2,1,0:T(8,128)S(1)} %get-tuple-element.833, f32[64,16,128]{2,1,0:T(8,128)S(1)} %get-tuple-element.832, f32[64,16,128]{2,1,0:T(8,128)S(1)} %get-tuple-element.831, f32[64,16,128]{2,1,0:T(8,128)S(1)} %get-tuple-element.830, ...), kind=kLoop, calls=%fused_computation.182.clone.1 | loop fusion | flops 10616832 | bytes 4194304 | tf_op jit(solution)/shard_map/while/body/eval_jaxpr/add | solution.py:84
  351.6 2.2 scatter_fusion
  355.6 10.8 %fusion.123 = (f32[64,16,128]{2,1,0:T(8,128)}, f32[64,16,128]{2,1,0:T(8,128)}) fusion(f32[64,16,128]{2,1,0:T(8,128)S(1)} %get-tuple-element.834, f32[64,16,128]{2,1,0:T(8,128)S(1)} %bitcast.104, f32[64,16,128]{2,1,0:T(8,128)} %dynamic-slice_bitcast_fusion.2, f32[64,16,128]{2,1,0:T(8,128)} %get-tuple-element.812, pred[]{:T(512)S(6)} %compare.60, ...), kind=kLoop, calls=%fused_computation.115.clone.1 | loop fusion | flops 10092544 | bytes 4194309 | tf_op jit(solution)/shard_map/while/body/eval_jaxpr/add | solution.py:92
  368.0 8.8 %multiply_add_fusion.8 = f32[64,16,128]{2,1,0:T(8,128)S(1)} fusion(f32[64,16,128]{2,1,0:T(8,128)S(1)} %get-tuple-element.834, f32[64,16,128]{2,1,0:T(8,128)S(1)} %get-tuple-element.833, f32[64,16,128]{2,1,0:T(8,128)S(1)} %get-tuple-element.832, f32[64,16,128]{2,1,0:T(8,128)S(1)} %get-tuple-element.831, f32[64,16,128]{2,1,0:T(8,128)S(1)} %get-tuple-element.830, ...), kind=kLoop, calls=%fused_computation.182.clone.1 | loop fusion | flops 10616832 | bytes 4194304 | tf_op jit(solution)/shard_map/while/body/eval_jaxpr/add | solution.py:84
  377.5 2.2 scatter_fusion
  381.6 10.8 %fusion.123 = (f32[64,16,128]{2,1,0:T(8,128)}, f32[64,16,128]{2,1,0:T(8,128)}) fusion(f32[64,16,128]{2,1,0:T(8,128)S(1)} %get-tuple-element.834, f32[64,16,128]{2,1,0:T(8,128)S(1)} %bitcast.104, f32[64,16,128]{2,1,0:T(8,128)} %dynamic-slice_bitcast_fusion.2, f32[64,16,128]{2,1,0:T(8,128)} %get-tuple-element.812, pred[]{:T(512)S(6)} %compare.60, ...), kind=kLoop, calls=%fused_computation.115.clone.1 | loop fusion | flops 10092544 | bytes 4194309 | tf_op jit(solution)/shard_map/while/body/eval_jaxpr/add | solution.py:92
  394.0 3.8 stack.9
  397.8 4.9 copy.34
  402.7 2.6 stack.10
  405.3 3.1 copy.35
  408.7 3.8 maximum_bitcast_fusion
  412.6 8.1 %reshape.319 = f32[32,2,4096]{2,0,1:T(8,128)S(1)} reshape(f32[4,8,2,16,16,16]{5,4,3,1,0,2:T(8,128)} %maximum_bitcast_fusion) | data formatting | bytes 2097152 | tf_op jit(solution)/shard_map/reshape | solution.py:58
  421.5 2.4 broadcast_in_dim.58
  423.8 4.6 scatter_fusion.1
  428.4 5.1 all-to-all-start.1
  434.9 47.3 %all-to-all-done.1 = f32[32,2,2,4096]{3,2,1,0:T(2,128)S(1)} async-done(((f32[32,2,2,4096]{3,2,1,0:T(2,128)}), f32[32,2,2,4096]{3,2,1,0:T(2,128)S(1)}, u32[]{:S(2)}, u32[]{:S(2)}) %all-to-all-start.1) | async-done | bytes 2097184 | tf_op jit(solution)/shard_map/all_to_all | solution.py:153
  482.2 2.8 fusion.75
  485.1 56.3 %reduce-scatter.2.cloned.1.call-done = f32[16,2,256]{2,0,1:T(8,128)} async-done(((f32[16,2,4096]{2,0,1:T(8,128)}), f32[16,2,256]{2,0,1:T(8,128)}) %reduce-scatter.2.cloned.1.call-update) | async-done | bytes 32784 | tf_op jit(solution)/shard_map/reduce_scatter | solution.py:164
  (138 shorter events, 40.5 us)
Async XLA Ops:
  6.5 1.4 copy-start
  6.5 113.6 %all-gather.2.cloned.1.call-start = ((), (), s32[]{:S(2)}) async-start(), calls=%async_computation.3 | async-start | bytes 8650752 | tf_op jit(solution)/shard_map/all_gather | solution.py:135
  9.7 418.8 %all-to-all-start = ((s32[32,1,2]{2,1,0:T(1,128)}), s32[32,1,2]{2,1,0:T(1,128)S(1)}, u32[]{:S(2)}, u32[]{:S(2)}) async-start(s32[32,1,2]{2,1,0:T(1,128)} %bitcast.7), calls=%async_computation | async-start | bytes 32768 | tf_op jit(solution)/shard_map/all_to_all | solution.py:154
  150.8 3.3 copy-start.7
  154.0 32.5 %copy-start.6 = (s32[1,256]{1,0:T(1,128)S(1)}, s32[1,256]{1,0:T(1,128)}, u32[]{:S(2)}) copy-start(s32[1,256]{1,0:T(1,128)} %param.22) | copy-start | bytes 3076
  154.2 2.9 copy-start.4
  158.3 2.8 copy-start.4
  162.3 2.9 copy-start.4
  166.4 2.9 copy-start.4
  170.4 2.8 copy-start.4
  174.4 2.8 copy-start.4
  178.5 2.9 copy-start.4
  182.5 2.9 copy-start.4
  200.1 10.6 %copy-start.2 = (f32[64,16,128]{2,1,0:T(8,128)S(1)}, f32[64,16,128]{2,1,0:T(8,128)}, u32[]{:S(2)}) copy-start(f32[64,16,128]{2,1,0:T(8,128)} %get-tuple-element.810) | copy-start | bytes 1572868 | tf_op jit(solution)/shard_map/while
  225.8 10.8 %copy-start.2 = (f32[64,16,128]{2,1,0:T(8,128)S(1)}, f32[64,16,128]{2,1,0:T(8,128)}, u32[]{:S(2)}) copy-start(f32[64,16,128]{2,1,0:T(8,128)} %get-tuple-element.810) | copy-start | bytes 1572868 | tf_op jit(solution)/shard_map/while
  251.8 10.8 %copy-start.2 = (f32[64,16,128]{2,1,0:T(8,128)S(1)}, f32[64,16,128]{2,1,0:T(8,128)}, u32[]{:S(2)}) copy-start(f32[64,16,128]{2,1,0:T(8,128)} %get-tuple-element.810) | copy-start | bytes 1572868 | tf_op jit(solution)/shard_map/while
  277.8 10.8 %copy-start.2 = (f32[64,16,128]{2,1,0:T(8,128)S(1)}, f32[64,16,128]{2,1,0:T(8,128)}, u32[]{:S(2)}) copy-start(f32[64,16,128]{2,1,0:T(8,128)} %get-tuple-element.810) | copy-start | bytes 1572868 | tf_op jit(solution)/shard_map/while
  303.7 10.8 %copy-start.2 = (f32[64,16,128]{2,1,0:T(8,128)S(1)}, f32[64,16,128]{2,1,0:T(8,128)}, u32[]{:S(2)}) copy-start(f32[64,16,128]{2,1,0:T(8,128)} %get-tuple-element.810) | copy-start | bytes 1572868 | tf_op jit(solution)/shard_map/while
  329.7 10.8 %copy-start.2 = (f32[64,16,128]{2,1,0:T(8,128)S(1)}, f32[64,16,128]{2,1,0:T(8,128)}, u32[]{:S(2)}) copy-start(f32[64,16,128]{2,1,0:T(8,128)} %get-tuple-element.810) | copy-start | bytes 1572868 | tf_op jit(solution)/shard_map/while
  355.6 10.8 %copy-start.2 = (f32[64,16,128]{2,1,0:T(8,128)S(1)}, f32[64,16,128]{2,1,0:T(8,128)}, u32[]{:S(2)}) copy-start(f32[64,16,128]{2,1,0:T(8,128)} %get-tuple-element.810) | copy-start | bytes 1572868 | tf_op jit(solution)/shard_map/while
  381.6 10.8 %copy-start.2 = (f32[64,16,128]{2,1,0:T(8,128)S(1)}, f32[64,16,128]{2,1,0:T(8,128)}, u32[]{:S(2)}) copy-start(f32[64,16,128]{2,1,0:T(8,128)} %get-tuple-element.810) | copy-start | bytes 1572868 | tf_op jit(solution)/shard_map/while
  397.8 4.9 copy-start.3
  405.3 3.4 copy-start.5
  423.8 118.9 %copy-start.1 = (s32[512]{0:T(512)S(1)}, s32[512]{0:T(512)}, u32[]{:S(2)}) copy-start(s32[512]{0:T(512)} %param.15) | copy-start | bytes 6148
  428.4 53.8 %all-to-all-start.1 = ((f32[32,2,2,4096]{3,2,1,0:T(2,128)}), f32[32,2,2,4096]{3,2,1,0:T(2,128)S(1)}, u32[]{:S(2)}, u32[]{:S(2)}) async-start(f32[32,2,2,4096]{3,2,1,0:T(2,128)} %bitcast.22), calls=%async_computation.1 | async-start | bytes 4194304 | tf_op jit(solution)/shard_map/all_to_all | solution.py:153
  433.6 107.8 %reduce-scatter.2.cloned.1.call-start = ((), (), s32[]{:S(2)}) async-start(), calls=%async_computation.4 | async-start | bytes 557056 | tf_op jit(solution)/shard_map/reduce_scatter | solution.py:164
Sparse Core Ops, SparseCore 0:
  10.5 109.5 all-gather.1
  485.2 56.1 reduce-scatter.1
where the time goes:
time: 552 us; the launch traced here: 550 us
  other arithmetic  212 us (38%)
  waiting for transfers between devices  196 us (36%)
  local copies, waits for them, and re-layouts  105 us (19%)
  starting transfers between devices  18.9 us (3%)
  between operations  14.3 us (3%)
    all_gather x1, waiting for transfers between devices, per_device(): shard_rows = lax.all_gather(model, 'tile', axis=0, tiled=True)  91.6 us
    add x8, other arithmetic, adjoint_step(): grad_gain = grad_gain + speed * product  86.2 us
    add x8, other arithmetic, adjoint_step(): 2.0 * current - later + speed * operate(current, gain_field, slopes)  70.2 us
    reduce_scatter x1, waiting for transfers between devices, per_device(): return lax.psum_scatter(owned_sum, 'shot', scatter_dimension=2, tiled=True)  56.3 us
    all_to_all x1, waiting for transfers between devices, per_device(): lax.all_to_all(outgoing, 'tile', split_axis=0, concat_axis=0, tiled=True)  47.3 us
    dynamic_update_slice x8, other arithmetic, evolve(): lax.scan(forward_step, (fwd_pair[0], fwd_pair[1]), pulses)  22.8 us
    while x64, local copies, waits for them, and re-layouts  19.6 us
    scatter-add x16, other arithmetic, inject(): return wave_field.reshape(-1).at[cells].add(amounts).reshape(volume_shape)  18.8 us
  transfers between devices with their start and end apart: 4, of which 3 were waited for; matrix products, arithmetic and copies ran while one was open for 57% of the time, Pallas kernels for 0%

commit v1 on v0

v1 whole, which is shorter than its diff:
```python
import jax
import jax.numpy as jnp
import ml_dtypes
import numpy as np
from jax import lax
from jax.experimental import pallas as pl
from jax.experimental.pallas import tpu as pltpu
from jax.sharding import PartitionSpec as P

B = 16
APX = 4
APZ = 8
NX, NY, NZ = 64, 16, 128
STEPS = 8
NREC = 256
COEF_SECOND = (-205.0 / 72.0, 8.0 / 5.0, -1.0 / 5.0, 8.0 / 315.0, -1.0 / 560.0)
COEF_FIRST = (4.0 / 5.0, -1.0 / 5.0, 4.0 / 105.0, -1.0 / 280.0)
SPEED_SCALE = 0.12
F32 = jnp.float32
BF16 = jnp.bfloat16
MESH = pl.DeviceIdType.MESH
PLANES = 16
UNROLL = 4
DEPTH_CHIPS = 8
TURNED = tuple((8 - i) % 8 for i in range(8))


def band(extent, centre):
    second = np.zeros((extent, extent))
    first = np.zeros((extent, extent))
    for to in range(extent):
        second[to, to] = centre
        for reach in range(1, 5):
            if to + reach < extent:
                second[to, to + reach] = COEF_SECOND[reach]
                first[to, to + reach] = COEF_FIRST[reach - 1]
            if to - reach >= 0:
                second[to, to - reach] = COEF_SECOND[reach]
                first[to, to - reach] = -COEF_FIRST[reach - 1]
    return second, first


def parts_of(matrix):
    high = matrix.astype(ml_dtypes.bfloat16)
    low = (matrix - high.astype(np.float64)).astype(ml_dtypes.bfloat16)
    return high, low


def depth_matrix():
    second, first = band(NZ, 3.0 * COEF_SECOND[0])
    high, low = parts_of(np.concatenate([second.T, first.T], axis=1))
    return np.concatenate([high, high, low], axis=0)


def middle_matrix():
    second, first = band(NY, 0.0)
    eight = np.eye(8)
    high, low = parts_of(np.concatenate([np.kron(eight, second), np.kron(eight, first)], axis=0))
    return np.concatenate([high, high, low], axis=1)


def split_two(values):
    high = values.astype(BF16)
    low = (values - high.astype(F32)).astype(BF16)
    return high, low


def turn(block, lane_block):
    block = pltpu.roll(block, 0, 1, stride=B, stride_axis=0)
    for bit in (1, 2, 4):
        block = jnp.where((lane_block & bit) != 0, pltpu.roll(block, 8 - bit, 0), block)
    return pltpu.roll(block, 0, 1, stride=B, stride_axis=0)


def derivatives(window, depth_ref, middle_ref):
    planes = window.shape[0] - 8
    inner = window[4 : 4 + planes].reshape(planes * NY, NZ)
    high, low = split_two(inner)
    along_depth = jnp.dot(
        jnp.concatenate([high, low, high], axis=1), depth_ref[...], preferred_element_type=F32
    )
    halves = range(planes // 8)
    stacked = jnp.concatenate(
        [
            jnp.concatenate([part[128 * h : 128 * h + 128] for h in halves], axis=1)
            for part in (high, low, high)
        ],
        axis=0,
    )
    along_middle = jnp.dot(middle_ref[...], stacked, preferred_element_type=F32)
    middle_second = jnp.concatenate([along_middle[:128, 128 * h : 128 * h + 128] for h in halves], axis=0)
    middle_first = jnp.concatenate([along_middle[128:, 128 * h : 128 * h + 128] for h in halves], axis=0)
    second = along_depth[:, :NZ] + middle_second
    first = None
    for reach in range(1, 5):
        ahead = window[4 + reach : 4 + reach + planes].reshape(planes * NY, NZ)
        behind = window[4 - reach : 4 - reach + planes].reshape(planes * NY, NZ)
        second = second + COEF_SECOND[reach] * (ahead + behind)
        term = COEF_FIRST[reach - 1] * (ahead - behind)
        first = term if first is None else first + term
    return second, first, middle_first, along_depth[:, NZ:]


def wave_kernel(
    tiles_ref, fwd_ref, adj_ref, source_ref, pulse_ref, cells_ref, traces_ref, depth_ref, middle_ref,
    out_ref,
    gain_ref, speed_ref, slope_ref, wave_ref, image_ref, first_ref, inject_ref, hot_ref, sums_ref,
):
    lane_block = lax.broadcasted_iota(jnp.int32, (8, NZ), 1) // B
    rows = PLANES * NY

    def flat(ref, at):
        return ref[pl.ds(at * PLANES, PLANES)].reshape(rows, NZ)

    def put(ref, at, values):
        ref[pl.ds(at * PLANES, PLANES)] = values.reshape(PLANES, NY, NZ)

    border = jnp.zeros((4, NY, NZ), F32)
    for ref in (gain_ref, wave_ref.at[0], wave_ref.at[1]):
        ref[0:4] = border
        ref[NX + 4 : NX + 8] = border

    def unpack(plane, carry):
        for block in range(APX):
            at = block * B + plane
            for field in range(2):
                for half in range(2):
                    lanes = (field * 2 + half) * NZ
                    rows_of = tiles_ref[plane, block * 8 : block * 8 + 8, lanes : lanes + NZ].astype(F32)
                    turned = turn(rows_of, lane_block)
                    if field == 0:
                        speed_ref[at, half * 8 : half * 8 + 8] = SPEED_SCALE * turned
                    else:
                        gain_ref[at + 4, half * 8 : half * 8 + 8] = turned
        return carry

    lax.fori_loop(0, B, unpack, 0)

    def slopes(at, carry):
        window = gain_ref[pl.ds(at * PLANES, PLANES + 8)]
        _, along_x, along_y, along_z = derivatives(window, depth_ref, middle_ref)
        put(slope_ref.at[0], at, along_x)
        put(slope_ref.at[1], at, along_y)
        put(slope_ref.at[2], at, along_z)
        return carry

    lax.fori_loop(0, NX // PLANES, slopes, 0)

    cells = cells_ref[...]
    cell_rows = lax.shift_right_logical(cells, 7)
    cell_lanes = jnp.transpose(jnp.broadcast_to((cells & 127).astype(F32), (8, NREC)))[:, 0:1]
    trace_columns = jnp.transpose(traces_ref[...])
    for at in range(8):
        row_ids = lax.broadcasted_iota(jnp.int32, (128, NREC), 0) + at * 128
        hot_ref[at * 128 : at * 128 + 128] = (row_ids == cell_rows).astype(F32).astype(BF16)
    lane_ids = lax.broadcasted_iota(jnp.int32, (NREC, NZ), 1).astype(F32)
    lane_hot = lane_ids == cell_lanes
    for step in range(STEPS):
        high, low = split_two(jnp.where(lane_hot, trace_columns[:, step : step + 1], 0.0))
        both = jnp.concatenate([high, low], axis=1)
        added = jnp.dot(hot_ref[...], both, preferred_element_type=F32)
        inject_ref[step] = (added[:, :NZ] + added[:, NZ:]).reshape(NX, NY, NZ)

    wave_ref[0, 4 : 4 + NX] = fwd_ref[0]
    wave_ref[1, 4 : 4 + NX] = fwd_ref[1]
    source = source_ref[0]
    source_x, source_y = source // (NY * NZ), (source // NZ) % NY
    source_lane = lax.broadcasted_iota(jnp.int32, (1, NZ), 1) == source % NZ

    def apply(window, at):
        second, along_x, along_y, along_z = derivatives(window, depth_ref, middle_ref)
        applied = flat(gain_ref.at[pl.ds(4, NX)], at) * second
        applied = applied + flat(slope_ref.at[0], at) * along_x
        applied = applied + flat(slope_ref.at[1], at) * along_y
        applied = applied + flat(slope_ref.at[2], at) * along_z
        return applied, along_x, along_y, along_z

    def forward(step, now):
        now_ref, other_ref = wave_ref.at[now], wave_ref.at[1 - now]

        def chunk(at, carry):
            window = now_ref[pl.ds(at * PLANES, PLANES + 8)]
            applied, along_x, along_y, along_z = apply(window, at)
            put(image_ref.at[step], at, applied)
            put(first_ref.at[step, 0], at, along_x)
            put(first_ref.at[step, 1], at, along_y)
            put(first_ref.at[step, 2], at, along_z)
            inner = other_ref.at[pl.ds(4, NX)]
            current = window[4 : 4 + PLANES].reshape(rows, NZ)
            put(inner, at, 2.0 * current - flat(inner, at) + flat(speed_ref, at) * applied)
            return carry

        lax.fori_loop(0, NX // PLANES, chunk, 0, unroll=UNROLL)
        line = other_ref[source_x + 4, pl.ds(source_y, 1)]
        other_ref[source_x + 4, pl.ds(source_y, 1)] = line + jnp.where(source_lane, pulse_ref[0, step], 0.0)

    def forward_pair(pair, carry):
        forward(2 * pair, 1)
        forward(2 * pair + 1, 0)
        return carry

    lax.fori_loop(0, STEPS // 2, forward_pair, 0)

    wave_ref[0, 4 : 4 + NX] = adj_ref[0]
    wave_ref[1, 4 : 4 + NX] = adj_ref[1]

    def backward(step, now, start):
        now_ref, other_ref = wave_ref.at[now], wave_ref.at[1 - now]

        def chunk(at, carry):
            window = now_ref[pl.ds(at * PLANES, PLANES + 8)]
            applied, along_x, along_y, along_z = apply(window, at)
            inner = other_ref.at[pl.ds(4, NX)]
            current = window[4 : 4 + PLANES].reshape(rows, NZ)
            newer = 2.0 * current - flat(inner, at) + flat(speed_ref, at) * applied
            newer = newer + flat(inject_ref.at[step], at)
            put(inner, at, newer)
            speed_part = newer * flat(image_ref.at[step], at)
            if start:
                put(sums_ref.at[0], at, speed_part)
                put(sums_ref.at[1], at, jnp.zeros((rows, NZ), F32))
            else:
                put(sums_ref.at[0], at, flat(sums_ref.at[0], at) + speed_part)
                part = flat(sums_ref.at[1], at) + along_x * flat(first_ref.at[step + 1, 0], at)
                part = part + along_y * flat(first_ref.at[step + 1, 1], at)
                part = part + along_z * flat(first_ref.at[step + 1, 2], at)
                put(sums_ref.at[1], at, part)
            return carry

        lax.fori_loop(0, NX // PLANES, chunk, 0, unroll=UNROLL)

    backward(STEPS - 1, 1, True)

    def backward_pair(pair, carry):
        backward(STEPS - 2 - 2 * pair, 0, False)
        backward(STEPS - 3 - 2 * pair, 1, False)
        return carry

    lax.fori_loop(0, STEPS // 2 - 1, backward_pair, 0)
    backward(0, 0, False)

    def last(at, carry):
        window = wave_ref[1, pl.ds(at * PLANES, PLANES + 8)]
        _, along_x, along_y, along_z = derivatives(window, depth_ref, middle_ref)
        part = flat(sums_ref.at[1], at) + along_x * flat(first_ref.at[0, 0], at)
        part = part + along_y * flat(first_ref.at[0, 1], at)
        part = part + along_z * flat(first_ref.at[0, 2], at)
        put(sums_ref.at[1], at, part * flat(speed_ref, at))
        return carry

    lax.fori_loop(0, NX // PLANES, last, 0, unroll=UNROLL)

    def pack(plane, carry):
        for block in range(APX):
            at = block * B + plane
            for field in range(2):
                for half in range(2):
                    lanes = (field * 2 + half) * NZ
                    values = sums_ref[field, at, half * 8 : half * 8 + 8]
                    out_ref[plane, block * 8 : block * 8 + 8, lanes : lanes + NZ] = turn(values, lane_block)
        return carry

    lax.fori_loop(0, B, pack, 0)


def wave(tiles, fwd, adj, source, pulses, cells, traces):
    vmem = pl.BlockSpec(memory_space=pltpu.VMEM)
    smem = pl.BlockSpec(memory_space=pltpu.SMEM)
    volume = (NX, NY, NZ)
    padded = (NX + 8, NY, NZ)
    return pl.pallas_call(
        wave_kernel,
        out_shape=jax.ShapeDtypeStruct((B, APX * APZ, 4 * NZ), F32),
        in_specs=[vmem, vmem, vmem, smem, smem, vmem, vmem, vmem, vmem],
        out_specs=vmem,
        scratch_shapes=[
            pltpu.VMEM(padded, F32),
            pltpu.VMEM(volume, F32),
            pltpu.VMEM((3,) + volume, F32),
            pltpu.VMEM((2,) + padded, F32),
            pltpu.VMEM((STEPS,) + volume, F32),
            pltpu.VMEM((STEPS, 3) + volume, F32),
            pltpu.VMEM((STEPS,) + volume, F32),
            pltpu.VMEM((NX * NY, NREC), BF16),
            pltpu.VMEM((2,) + volume, F32),
        ],
        compiler_params=pltpu.CompilerParams(vmem_limit_bytes=56 * 1024 * 1024),
        cost_estimate=pl.CostEstimate(flops=10**9, bytes_accessed=5 * 2**20, transcendentals=0),
        name="wave",
    )(tiles, fwd, adj, source, pulses, cells, traces, jnp.asarray(depth_matrix()), jnp.asarray(middle_matrix()))


def place():
    shot, tile = lax.axis_index("shot"), lax.axis_index("tile")
    shots, depths = lax.axis_size("shot"), DEPTH_CHIPS
    across = lax.axis_size("tile") // depths
    return shot, lax.div(tile, depths), lax.rem(tile, depths), shots, across, depths


def shifted(index, by, size):
    return lax.rem(index + by, size)


def greet(shot, x, z, shots, across, depths):
    barrier = pltpu.get_barrier_semaphore()

    def signal(device_id):
        pl.semaphore_signal(barrier, inc=1, device_id=device_id, device_id_type=MESH)

    def to_shot(by, carry):
        signal((shifted(shot, by, shots), x * depths + z))
        return carry

    lax.fori_loop(1, shots, to_shot, 0)
    for by in range(1, across):
        signal((shot, shifted(x, by, across) * depths + z))
    for by in range(1, depths):
        signal((shot, x * depths + shifted(z, by, depths)))
    pl.semaphore_wait(barrier, shots + across + depths - 3)


def remote(src, dst, send_sem, recv_sem, device_id):
    return pltpu.make_async_remote_copy(
        src_ref=src, dst_ref=dst, send_sem=send_sem, recv_sem=recv_sem,
        device_id=device_id, device_id_type=MESH,
    )


def rows_at(start, size):
    return pl.ds(pl.multiple_of(start, size), size)


def fetch_kernel(
    block_ref, names_ref,
    tiles_ref, groups_ref,
    store_ref, pick_ref, names_all, outgoing, incoming,
    z_send, z_recv, x_send, x_recv, name_send, name_recv, shot_send, shot_recv,
):
    shot, x, z, shots, across, depths = place()
    owned = block_ref.shape[0]
    me = x * depths + z
    greet(shot, x, z, shots, across, depths)

    store_ref[rows_at(me * owned, owned)] = block_ref[...]
    names_all[shot] = names_ref[...]

    def z_copy(by):
        return remote(
            block_ref, store_ref.at[rows_at(me * owned, owned)], z_send.at[by], z_recv.at[by],
            (shot, x * depths + shifted(z, by, depths)),
        )

    def name_copy(by):
        return remote(
            names_ref, names_all.at[shot], name_send.at[by], name_recv.at[by],
            (shifted(shot, by, shots), me),
        )

    def x_copy(along, by):
        rows = store_ref.at[rows_at((x * depths + shifted(z, depths - by, depths)) * owned, owned)]
        return remote(
            rows, rows, x_send.at[along, by], x_recv.at[along, by],
            (shot, shifted(x, along, across) * depths + z),
        )

    def start_z(by, carry):
        z_copy(by).start()
        return carry

    def start_name(by, carry):
        name_copy(by).start()
        return carry

    def pass_on(by, carry):
        z_copy(by).wait_recv()
        for along in range(1, across):
            x_copy(along, by).start()
        return carry

    lax.fori_loop(1, depths, start_z, 0)
    for along in range(1, across):
        x_copy(along, 0).start()
    lax.fori_loop(1, shots, start_name, 0)
    lax.fori_loop(1, depths, pass_on, 0)

    def wait_name(by, carry):
        name_copy(by).wait_recv()
        return carry

    lax.fori_loop(1, shots, wait_name, 0)

    group = NZ // (APX * APZ)
    lines, turned = [], []
    for at in range(8):
        if at < shots // group:
            lines.append(sum(names_all[group * at + i, 0:1] for i in range(group)))
            turned.append(sum(names_all[group * at + i, 1:2] for i in range(group)))
        else:
            lines.append(jnp.zeros((1, NZ), F32))
            turned.append(jnp.zeros((1, NZ), F32))
    groups_ref[...] = jnp.concatenate(turned, axis=0)
    columns = jnp.transpose(jnp.concatenate(lines, axis=0))
    total = store_ref.shape[0]
    row_ids = lax.broadcasted_iota(jnp.int32, (NZ, total), 1).astype(F32)
    for at in range(shots // group):
        pick_ref[at] = (row_ids == columns[:, at : at + 1]).astype(F32).astype(BF16)

    def wait_x(by, carry):
        for along in range(1, across):
            x_copy(along, by).wait_recv()
        return carry

    lax.fori_loop(0, depths, wait_x, 0)

    def choose(at, carry):
        chosen = jnp.dot(pick_ref[at], store_ref[...], preferred_element_type=F32).astype(BF16)
        outgoing[pl.ds(at * group, group)] = chosen.reshape(group, APX * APZ, chosen.shape[1])
        return carry

    lax.fori_loop(0, shots // group, choose, 0)

    def shot_copy(by):
        target = shifted(shot, by, shots)
        return remote(
            outgoing.at[target], incoming.at[shot], shot_send.at[by], shot_recv.at[by], (target, me)
        )

    def start_shot(by, carry):
        shot_copy(by).start()
        return carry

    lax.fori_loop(1, shots, start_shot, 0)
    incoming[shot] = outgoing[shot]

    def finish_shot(by, carry):
        shot_copy(by).wait_recv()
        return carry

    lax.fori_loop(1, shots, finish_shot, 0)
    tiles_ref[...] = incoming[...]

    def finish_sends(by, carry):
        shot_copy(by).wait_send()
        name_copy(by).wait_send()
        return carry

    lax.fori_loop(1, shots, finish_sends, 0)

    def finish_z(by, carry):
        z_copy(by).wait_send()
        return carry

    lax.fori_loop(1, depths, finish_z, 0)

    def finish_x(by, carry):
        for along in range(1, across):
            x_copy(along, by).wait_send()
        return carry

    lax.fori_loop(0, depths, finish_x, 0)


def fetch(block, names, shots, tiles):
    vmem = pl.BlockSpec(memory_space=pltpu.VMEM)
    owned, cells = block.shape
    across = tiles // DEPTH_CHIPS
    group = NZ // (APX * APZ)
    dma = pltpu.SemaphoreType.DMA
    return pl.pallas_call(
        fetch_kernel,
        out_shape=(
            jax.ShapeDtypeStruct((shots, APX * APZ, cells), BF16),
            jax.ShapeDtypeStruct((8, NZ), F32),
        ),
        in_specs=[vmem, vmem],
        out_specs=(vmem, vmem),
        scratch_shapes=[
            pltpu.VMEM((tiles * owned, cells), BF16),
            pltpu.VMEM((shots // group, NZ, tiles * owned), BF16),
            pltpu.VMEM((shots, 8, NZ), F32),
            pltpu.VMEM((shots, APX * APZ, cells), BF16),
            pltpu.VMEM((shots, APX * APZ, cells), BF16),
            dma((DEPTH_CHIPS,)), dma((DEPTH_CHIPS,)),
            dma((across, DEPTH_CHIPS)), dma((across, DEPTH_CHIPS)),
            dma((shots,)), dma((shots,)), dma((shots,)), dma((shots,)),
        ],
        compiler_params=pltpu.CompilerParams(
            collective_id=0, has_side_effects=True, vmem_limit_bytes=32 * 1024 * 1024
        ),
        cost_estimate=pl.CostEstimate(flops=3 * 10**8, bytes_accessed=2**21, transcendentals=0),
        name="fetch",
    )(block, names)


def collect_kernel(
    grads_ref, groups_ref,
    out_ref,
    incoming, place_ref, whole, from_x, column, from_z,
    shot_send, shot_recv, x_send, x_recv, z_send, z_recv,
):
    shot, x, z, shots, across, depths = place()
    owned = out_ref.shape[0]
    me = x * depths + z
    greet(shot, x, z, shots, across, depths)

    def shot_copy(by):
        target = shifted(shot, by, shots)
        return remote(
            grads_ref.at[target], incoming.at[shot], shot_send.at[by], shot_recv.at[by], (target, me)
        )

    def start_shot(by, carry):
        shot_copy(by).start()
        return carry

    lax.fori_loop(1, shots, start_shot, 0)
    incoming[shot] = grads_ref[shot]

    group = NZ // (APX * APZ)
    total = whole.shape[0]
    row_ids = lax.broadcasted_iota(jnp.int32, (total, NZ), 0).astype(F32)
    for at in range(shots // group):
        hot = (row_ids == groups_ref[at : at + 1]).astype(F32).astype(BF16)
        place_ref[at, :, :NZ] = hot
        place_ref[at, :, NZ:] = hot

    def finish_shot(by, carry):
        shot_copy(by).wait_recv()
        return carry

    lax.fori_loop(1, shots, finish_shot, 0)

    for at in range(shots // group):
        part = incoming[group * at : group * at + group].reshape(NZ, incoming.shape[2])
        high, low = split_two(part)
        added = jnp.dot(
            place_ref[at], jnp.concatenate([high, low], axis=0), preferred_element_type=F32
        )
        whole[...] = added if at == 0 else whole[...] + added

    def x_copy(along):
        target = shifted(x, along, across)
        return remote(
            whole.at[rows_at(target * depths * owned, depths * owned)], from_x.at[along],
            x_send.at[along], x_recv.at[along], (shot, target * depths + z),
        )

    for along in range(1, across):
        x_copy(along).start()
    for along in range(1, across):
        x_copy(along).wait_recv()
    summed = whole[rows_at(x * depths * owned, depths * owned)]
    for along in range(1, across):
        summed = summed + from_x[along]
    column[...] = summed

    def z_copy(by):
        target = shifted(z, by, depths)
        return remote(
            column.at[rows_at(target * owned, owned)], from_z.at[by],
            z_send.at[by], z_recv.at[by], (shot, x * depths + target),
        )

    for by in range(1, depths):
        z_copy(by).start()
    for by in range(1, depths):
        z_copy(by).wait_recv()
    mine = column[rows_at(z * owned, owned)]
    for by in range(1, depths):
        mine = mine + from_z[by]
    out_ref[...] = mine

    def finish_sends(by, carry):
        shot_copy(by).wait_send()
        return carry

    lax.fori_loop(1, shots, finish_sends, 0)
    for along in range(1, across):
        x_copy(along).wait_send()
    for by in range(1, depths):
        z_copy(by).wait_send()


def collect(grads, groups, tiles, owned):
    vmem = pl.BlockSpec(memory_space=pltpu.VMEM)
    shots, _, cells = grads.shape
    across = tiles // DEPTH_CHIPS
    group = NZ // (APX * APZ)
    dma = pltpu.SemaphoreType.DMA
    return pl.pallas_call(
        collect_kernel,
        out_shape=jax.ShapeDtypeStruct((owned, cells), F32),
        in_specs=[vmem, vmem],
        out_specs=vmem,
        scratch_shapes=[
            pltpu.VMEM((shots, APX * APZ, cells), F32),
            pltpu.VMEM((shots // group, tiles * owned, 2 * NZ), BF16),
            pltpu.VMEM((tiles * owned, cells), F32),
            pltpu.VMEM((across, DEPTH_CHIPS * owned, cells), F32),
            pltpu.VMEM((DEPTH_CHIPS * owned, cells), F32),
            pltpu.VMEM((DEPTH_CHIPS, owned, cells), F32),
            dma((shots,)), dma((shots,)), dma((across,)), dma((across,)),
            dma((DEPTH_CHIPS,)), dma((DEPTH_CHIPS,)),
        ],
        compiler_params=pltpu.CompilerParams(
            collective_id=1, has_side_effects=True, vmem_limit_bytes=32 * 1024 * 1024
        ),
        cost_estimate=pl.CostEstimate(flops=5 * 10**8, bytes_accessed=2**21, transcendentals=0),
        name="collect",
    )(grads, groups)


def per_device(
    tile_store, apertures, model, fwd_states, adj_states, source_cell, wavelet, receiver_cells, residuals
):
    shot = lax.axis_index("shot")
    shots, tiles = lax.axis_size("shot"), lax.axis_size("tile")
    owned = model.shape[0]
    positions = APX * APZ
    cells = model.shape[2] // shots

    rows = tile_store[apertures[0]].astype(F32)
    turned = rows.reshape(APX, APZ)
    turned = jnp.concatenate([turned[:, :1], turned[:, :0:-1]], axis=1).reshape(positions)
    group = NZ // positions
    mine = jnp.repeat(jnp.arange(group) == lax.rem(shot, group), positions)
    lines = [jnp.where(mine, jnp.tile(line, group), 0.0) for line in (rows, turned)]
    names = jnp.concatenate([jnp.stack(lines), jnp.zeros((6, NZ), F32)])

    block = lax.dynamic_slice_in_dim(model, shot * cells, cells, axis=2)
    block = block.reshape(owned, 4, 8, B)
    block = jnp.concatenate([block[:, :, :1], block[:, :, :0:-1]], axis=2).reshape(owned, 2 * cells)

    fetched, groups = fetch(block, names, shots, tiles)
    grads = wave(
        fetched, fwd_states[0], adj_states[0], source_cell, wavelet, receiver_cells, residuals[0]
    )
    return collect(grads, groups, tiles, owned).reshape(owned, 2, cells)


def solution(mesh):
    return jax.shard_map(
        per_device,
        mesh=mesh,
        in_specs=(
            P(),
            P(("shot", "tile"), None),
            P("tile", None, None),
            P(("shot", "tile"), None, None, None, None),
            P(("shot", "tile"), None, None, None, None),
            P(("shot", "tile")),
            P(("shot", "tile"), None),
            P(("shot", "tile"), None),
            P(("shot", "tile"), None, None),
        ),
        out_specs=P("tile", None, "shot"),
        check_vma=False,
    )
```

time: 552 us -> 131 us (0.24)
  other arithmetic: 212 us -> 0.34 us
  waiting for transfers between devices: 196 us -> 0 us
  Pallas kernels: 0 us -> 124 us
  local copies, waits for them, and re-layouts: 105 us -> 5.81 us
  starting transfers between devices: 18.9 us -> 0 us
  between operations: 14.3 us -> 0.79 us
    add x28 -> x0, other arithmetic: 159 us -> none  [the longest x8 86.2 us: adjoint_step(): grad_gain = grad_gain + speed * product]
    pallas_call x0 -> x3, Pallas kernels: none -> 124 us  [the longest x1 55.1 us: collect(): pl.pallas_call(collect_kernel, out_shape=jax.ShapeDtypeStruct((owned, cel...]
    all_gather x1 -> x0, waiting for transfers between devices: 91.6 us -> none  [per_device(): shard_rows = lax.all_gather(model, 'tile', axis=0, tiled=True)]
    reduce_scatter x1 -> x0, waiting for transfers between devices: 56.3 us -> none  [per_device(): return lax.psum_scatter(owned_sum, 'shot', scatter_dimension=2, tiled=True)]
    all_to_all x2 -> x0, waiting for transfers between devices: 47.3 us -> none  [the longest x1 47.3 us: per_device(): lax.all_to_all(outgoing, 'tile', split_axis=0, concat_axis=0, tiled=True)]
    dynamic_update_slice x8 -> x0, other arithmetic: 22.8 us -> none  [evolve(): lax.scan(forward_step, (fwd_pair[0], fwd_pair[1]), pulses)]
    squeeze x11 -> x0, local copies, waits for them, and re-layouts: 22.5 us -> none  [the longest x8 15 us: evolve(): lax.scan(adjoint_step, (adj_pair[0], adj_pair[1], zeros_field, zeros_fiel...]
    while x64 -> x0, local copies, waits for them, and re-layouts: 19.6 us -> none
  transfers between devices with their start and end apart: 4 -> 0, of which waited for: 3 -> 0; matrix products, arithmetic and copies ran while one was open for 57% -> 0% of each run, Pallas kernels for 0% -> 0%
where the time goes in v1:
time: 131 us
  Pallas kernels  124 us (95%)
  local copies, waits for them, and re-layouts  5.81 us (4%)
    pallas_call x1, Pallas kernels, collect(): pl.pallas_call(collect_kernel, out_shape=jax.ShapeDtypeStruct((owned, cel...  55.1 us
    pallas_call x1, Pallas kernels, fetch(): pl.pallas_call(fetch_kernel, out_shape=(jax.ShapeDtypeStruct((shots, APX...  40.9 us
    pallas_call x1, Pallas kernels, wave(): pl.pallas_call(wave_kernel, out_shape=jax.ShapeDtypeStruct((B, APX * APZ,...  27.9 us
    unnamed x10, local copies, waits for them, and re-layouts  3.35 us

profile of v1, /device:TPU:1, one launch (start us, length us, event | category | flops | bytes accessed | tf_op | source)
XLA Modules:
  0.0 130.9 jit_solution(7408846057143052856)
XLA Ops:
  0.0 0.0 copy-start
  0.7 0.0 copy-start.4
  0.7 0.6 copy-done.4
  1.4 0.1 pad.2.clone
  1.5 0.0 copy-start.3
  1.5 0.7 copy-done.3
  2.1 0.7 gather_fusion
  2.9 0.1 convert_element_type.12
  2.9 0.1 slice.15
  3.0 0.1 rev.7
  3.1 0.1 pad_maximum_fusion.1
  3.2 0.1 tile.7
  3.3 0.1 broadcast_select_fusion.1
  3.3 0.1 select_n.43
  3.4 0.1 select_n.45
  3.5 0.1 maximum_maximum_fusion.names_ref
  3.6 0.0 copy-done
  3.6 0.1 reshape.83
  3.8 0.1 rev.6
  4.0 0.1 pad_maximum_fusion
  4.1 0.2 reshape.84.block_ref
  4.2 40.9 %fetch.1 = (bf16[16,32,512]{2,1,0:T(8,128)(2,1)S(1)}, f32[8,128]{1,0:T(8,128)S(1)}) custom-call(bf16[16,512]{1,0:T(8,128)(2,1)S(1)} %reshape.84.block_ref, f32[8,128]{1,0:T(8,128)S(1)} %maximum_maximum_fusion.names_ref), custom_call_target="tpu_custom_call" | custom-call | flops 300000000 | bytes 2097152 | tf_op jit(solution)/shard_map/fetch/pallas_call | solution.py:469
  45.2 0.0 copy-start.2
  45.2 0.8 copy-done.2
  46.0 27.9 %wave.1.grads_ref = f32[16,32,512]{2,1,0:T(8,128)} custom-call(bf16[16,32,512]{2,1,0:T(8,128)(2,1)} %copy-done.2, f32[2,64,16,128]{3,2,1,0:T(8,128)} %bitcast.10, f32[2,64,16,128]{3,2,1,0:T(8,128)} %bitcast.11, s32[1]{0:T(128)S(6)} %copy.12.source_ref, f32[1,8]{1,0:T(1,128)} %pulse_ref.1, s32[1,256]{1,0:T(1,128)} %cells_ref.1, f32[8,256]{1,0:T(8,128)} %bitcast.13, ...), custom_call_target="tpu_custom_call" | custom-call | flops 1000000000 | bytes 5242880 | tf_op jit(solution)/shard_map/wave/pallas_call | solution.py:271
  73.9 0.0 copy-start.1
  73.9 1.2 copy-done.1
  75.1 55.1 %collect.1 = f32[16,512]{1,0:T(8,128)S(1)} custom-call(f32[16,32,512]{2,1,0:T(8,128)S(1)} %copy-done.1, f32[8,128]{1,0:T(8,128)S(1)} %get-tuple-element.8.groups_ref), custom_call_target="tpu_custom_call" | custom-call | flops 500000000 | bytes 2097152 | tf_op jit(solution)/shard_map/collect/pallas_call | solution.py:590
  130.2 0.6 reshape.85
  (8 shorter events, 0.1 us)
Async XLA Ops:
  0.0 3.6 %copy-start = (bf16[16,2,4096]{2,1,0:T(2,128)(2,1)S(1)}, bf16[16,2,4096]{2,1,0:T(2,128)(2,1)}, u32[]{:S(2)}) copy-start(bf16[16,2,4096]{2,1,0:T(2,128)(2,1)} %param.13) | copy-start | bytes 786436
  0.7 0.7 copy-start.4
  1.5 0.7 copy-start.3
  45.2 0.8 copy-start.2
  73.9 1.2 copy-start.1

commit v2 on v1

--- a/solution.py
+++ b/solution.py
@@ -18,6 +18,8 @@
 SPEED_SCALE = 0.12
 F32 = jnp.float32
 BF16 = jnp.bfloat16
+LEVELS = 32767.0
+SMALLEST = 1e-30
 MESH = pl.DeviceIdType.MESH
 PLANES = 16
 UNROLL = 4
@@ -63,6 +65,10 @@
     high = values.astype(BF16)
     low = (values - high.astype(F32)).astype(BF16)
     return high, low
+
+
+def to_levels(values):
+    return jnp.round(values).astype(jnp.int32).astype(jnp.int16)
 
 
 def turn(block, lane_block):
@@ -103,7 +109,7 @@
 
 def wave_kernel(
     tiles_ref, fwd_ref, adj_ref, source_ref, pulse_ref, cells_ref, traces_ref, depth_ref, middle_ref,
-    out_ref,
+    out_ref, unit_ref,
     gain_ref, speed_ref, slope_ref, wave_ref, image_ref, first_ref, inject_ref, hot_ref, sums_ref,
 ):
     lane_block = lax.broadcasted_iota(jnp.int32, (8, NZ), 1) // B
@@ -251,13 +257,25 @@
     lax.fori_loop(0, NX // PLANES, last, 0, unroll=UNROLL)
 
     def pack(plane, carry):
-        for block in range(APX):
-            at = block * B + plane
-            for field in range(2):
+        for field in range(2):
+            for pair in range(APX // 2):
+                coded = [[], []]
+                for block in (2 * pair, 2 * pair + 1):
+                    at = block * B + plane
+                    values = [sums_ref[field, at, half * 8 : half * 8 + 8] for half in range(2)]
+                    largest = jnp.maximum(jnp.abs(values[0]), jnp.abs(values[1]))
+                    largest = jnp.maximum(jnp.max(largest, axis=(0, 1), keepdims=True), SMALLEST)
+                    unit_ref[plane, field * APX + block : field * APX + block + 1] = (
+                        jnp.broadcast_to(largest * (1.0 / LEVELS), (1, NZ))
+                    )
+                    levels = LEVELS / largest
+                    for half in range(2):
+                        coded[half].append(turn(values[half] * levels, lane_block))
                 for half in range(2):
                     lanes = (field * 2 + half) * NZ
-                    values = sums_ref[field, at, half * 8 : half * 8 + 8]
-                    out_ref[plane, block * 8 : block * 8 + 8, lanes : lanes + NZ] = turn(values, lane_block)
+                    out_ref[plane, pair * 16 : pair * 16 + 16, lanes : lanes + NZ] = to_levels(
+                        jnp.concatenate(coded[half], axis=0)
+                    )
         return carry
 
     lax.fori_loop(0, B, pack, 0)
@@ -270,9 +288,12 @@
     padded = (NX + 8, NY, NZ)
     return pl.pallas_call(
         wave_kernel,
-        out_shape=jax.ShapeDtypeStruct((B, APX * APZ, 4 * NZ), F32),
+        out_shape=(
+            jax.ShapeDtypeStruct((B, APX * APZ, 4 * NZ), jnp.int16),
+            jax.ShapeDtypeStruct((B, 8, NZ), F32),
+        ),
         in_specs=[vmem, vmem, vmem, smem, smem, vmem, vmem, vmem, vmem],
-        out_specs=vmem,
+        out_specs=(vmem, vmem),
         scratch_shapes=[
             pltpu.VMEM(padded, F32),
             pltpu.VMEM(volume, F32),
@@ -492,11 +513,35 @@
     )(block, names)
 
 
+def row_levels(values):
+    rows, lanes = values.shape
+    field = lanes // 2
+    units, coded = [], []
+    for at in range(2):
+        part = values[:, at * field : (at + 1) * field]
+        largest = jnp.maximum(jnp.max(jnp.abs(part), axis=1, keepdims=True), SMALLEST)
+        units.append(largest * (1.0 / LEVELS))
+        coded.append(part * (LEVELS / largest))
+    first = lax.broadcasted_iota(jnp.int32, (rows, NZ), 1) == 0
+    lines = jnp.transpose(jnp.where(first, units[0], units[1]))[:8]
+    return to_levels(jnp.concatenate(coded, axis=1)), lines
+
+
+def from_levels(levels, units):
+    field = levels.shape[1] // 2
+    values = levels.astype(F32)
+    return jnp.concatenate(
+        [values[:, :field] * units[:, 0:1], values[:, field:] * units[:, 1:2]], axis=1
+    )
+
+
 def collect_kernel(
-    grads_ref, groups_ref,
+    grads_ref, units_ref, groups_ref,
     out_ref,
-    incoming, place_ref, whole, from_x, column, from_z,
-    shot_send, shot_recv, x_send, x_recv, z_send, z_recv,
+    incoming, units_all, place_ref, whole, whole_levels, whole_lines, from_x, lines_x,
+    column, column_levels, column_lines, from_z, lines_z, turned_units,
+    shot_send, shot_recv, unit_send, unit_recv, x_send, x_recv, xu_send, xu_recv,
+    z_send, z_recv, zu_send, zu_recv,
 ):
     shot, x, z, shots, across, depths = place()
     owned = out_ref.shape[0]
@@ -509,12 +554,20 @@
             grads_ref.at[target], incoming.at[shot], shot_send.at[by], shot_recv.at[by], (target, me)
         )
 
+    def unit_copy(by):
+        target = shifted(shot, by, shots)
+        return remote(
+            units_ref.at[target], units_all.at[shot], unit_send.at[by], unit_recv.at[by], (target, me)
+        )
+
     def start_shot(by, carry):
         shot_copy(by).start()
+        unit_copy(by).start()
         return carry
 
     lax.fori_loop(1, shots, start_shot, 0)
     incoming[shot] = grads_ref[shot]
+    units_all[shot] = units_ref[shot]
 
     group = NZ // (APX * APZ)
     total = whole.shape[0]
@@ -526,88 +579,143 @@
 
     def finish_shot(by, carry):
         shot_copy(by).wait_recv()
+        unit_copy(by).wait_recv()
         return carry
 
     lax.fori_loop(1, shots, finish_shot, 0)
 
     for at in range(shots // group):
-        part = incoming[group * at : group * at + group].reshape(NZ, incoming.shape[2])
-        high, low = split_two(part)
+        parts = []
+        for member in range(group * at, group * at + group):
+            levels = incoming[member].astype(F32)
+            for block in range(APX):
+                rows = levels[8 * block : 8 * block + 8]
+                parts.append(
+                    jnp.concatenate(
+                        [
+                            rows[:, lanes * NZ : lanes * NZ + NZ]
+                            * units_all[member, (lanes // 2) * APX + block : (lanes // 2) * APX + block + 1]
+                            for lanes in range(4)
+                        ],
+                        axis=1,
+                    )
+                )
+        high, low = split_two(jnp.concatenate(parts, axis=0))
         added = jnp.dot(
             place_ref[at], jnp.concatenate([high, low], axis=0), preferred_element_type=F32
         )
         whole[...] = added if at == 0 else whole[...] + added
 
+    block = depths * owned
+    for at in range(across):
+        coded, lines = row_levels(whole[at * block : (at + 1) * block])
+        whole_levels[at * block : (at + 1) * block] = coded
+        whole_lines[at] = lines
+
     def x_copy(along):
         target = shifted(x, along, across)
         return remote(
-            whole.at[rows_at(target * depths * owned, depths * owned)], from_x.at[along],
+            whole_levels.at[rows_at(target * block, block)], from_x.at[along],
             x_send.at[along], x_recv.at[along], (shot, target * depths + z),
+        )
+
+    def x_lines(along):
+        target = shifted(x, along, across)
+        return remote(
+            whole_lines.at[target], lines_x.at[along],
+            xu_send.at[along], xu_recv.at[along], (shot, target * depths + z),
         )
 
     for along in range(1, across):
         x_copy(along).start()
+        x_lines(along).start()
+    summed = whole[rows_at(x * block, block)]
     for along in range(1, across):
         x_copy(along).wait_recv()
-    summed = whole[rows_at(x * depths * owned, depths * owned)]
-    for along in range(1, across):
-        summed = summed + from_x[along]
+        x_lines(along).wait_recv()
+        summed = summed + from_levels(from_x[along], jnp.transpose(lines_x[along]))
     column[...] = summed
+    coded, lines = row_levels(summed)
+    column_levels[...] = coded
+    column_lines[...] = lines
 
     def z_copy(by):
         target = shifted(z, by, depths)
         return remote(
-            column.at[rows_at(target * owned, owned)], from_z.at[by],
+            column_levels.at[rows_at(target * owned, owned)], from_z.at[by],
             z_send.at[by], z_recv.at[by], (shot, x * depths + target),
+        )
+
+    def z_lines(by):
+        target = shifted(z, by, depths)
+        return remote(
+            column_lines, lines_z.at[by], zu_send.at[by], zu_recv.at[by], (shot, x * depths + target)
         )
 
     for by in range(1, depths):
         z_copy(by).start()
+        z_lines(by).start()
+    mine = column[rows_at(z * owned, owned)]
     for by in range(1, depths):
         z_copy(by).wait_recv()
-    mine = column[rows_at(z * owned, owned)]
-    for by in range(1, depths):
-        mine = mine + from_z[by]
+        z_lines(by).wait_recv()
+        turned_units[by] = jnp.transpose(lines_z[by])
+        mine = mine + from_levels(from_z[by], turned_units[by, rows_at(z * owned, owned)])
     out_ref[...] = mine
 
     def finish_sends(by, carry):
         shot_copy(by).wait_send()
+        unit_copy(by).wait_send()
         return carry
 
     lax.fori_loop(1, shots, finish_sends, 0)
     for along in range(1, across):
         x_copy(along).wait_send()
+        x_lines(along).wait_send()
     for by in range(1, depths):
         z_copy(by).wait_send()
-
-
-def collect(grads, groups, tiles, owned):
+        z_lines(by).wait_send()
+
+
+def collect(grads, units, groups, tiles, owned):
     vmem = pl.BlockSpec(memory_space=pltpu.VMEM)
     shots, _, cells = grads.shape
-    across = tiles // DEPTH_CHIPS
+    depths = DEPTH_CHIPS
+    across = tiles // depths
+    block = depths * owned
     group = NZ // (APX * APZ)
     dma = pltpu.SemaphoreType.DMA
+    int16 = jnp.int16
     return pl.pallas_call(
         collect_kernel,
         out_shape=jax.ShapeDtypeStruct((owned, cells), F32),
-        in_specs=[vmem, vmem],
+        in_specs=[vmem, vmem, vmem],
         out_specs=vmem,
         scratch_shapes=[
-            pltpu.VMEM((shots, APX * APZ, cells), F32),
+            pltpu.VMEM((shots, APX * APZ, cells), int16),
+            pltpu.VMEM((shots, 8, NZ), F32),
             pltpu.VMEM((shots // group, tiles * owned, 2 * NZ), BF16),
             pltpu.VMEM((tiles * owned, cells), F32),
-            pltpu.VMEM((across, DEPTH_CHIPS * owned, cells), F32),
-            pltpu.VMEM((DEPTH_CHIPS * owned, cells), F32),
-            pltpu.VMEM((DEPTH_CHIPS, owned, cells), F32),
-            dma((shots,)), dma((shots,)), dma((across,)), dma((across,)),
-            dma((DEPTH_CHIPS,)), dma((DEPTH_CHIPS,)),
+            pltpu.VMEM((tiles * owned, cells), int16),
+            pltpu.VMEM((across, 8, block), F32),
+            pltpu.VMEM((across, block, cells), int16),
+            pltpu.VMEM((across, 8, block), F32),
+            pltpu.VMEM((block, cells), F32),
+            pltpu.VMEM((block, cells), int16),
+            pltpu.VMEM((8, block), F32),
+            pltpu.VMEM((depths, owned, cells), int16),
+            pltpu.VMEM((depths, 8, block), F32),
+            pltpu.VMEM((depths, block, 8), F32),
+            dma((shots,)), dma((shots,)), dma((shots,)), dma((shots,)),
+            dma((across,)), dma((across,)), dma((across,)), dma((across,)),
+            dma((depths,)), dma((depths,)), dma((depths,)), dma((depths,)),
         ],
         compiler_params=pltpu.CompilerParams(
             collective_id=1, has_side_effects=True, vmem_limit_bytes=32 * 1024 * 1024
         ),
         cost_estimate=pl.CostEstimate(flops=5 * 10**8, bytes_accessed=2**21, transcendentals=0),
         name="collect",
-    )(grads, groups)
+    )(grads, units, groups)
 
 
 def per_device(
@@ -632,10 +740,10 @@
     block = jnp.concatenate([block[:, :, :1], block[:, :, :0:-1]], axis=2).reshape(owned, 2 * cells)
 
     fetched, groups = fetch(block, names, shots, tiles)
-    grads = wave(
+    grads, units = wave(
         fetched, fwd_states[0], adj_states[0], source_cell, wavelet, receiver_cells, residuals[0]
     )
-    return collect(grads, groups, tiles, owned).reshape(owned, 2, cells)
+    return collect(grads, units, groups, tiles, owned).reshape(owned, 2, cells)
 
 
 def solution(mesh):

time: 131 us -> 117 us (0.89)
  Pallas kernels: 124 us -> 110 us
    pallas_call x1, Pallas kernels: 55.1 us -> 38.6 us  [collect(): pl.pallas_call(collect_kernel, out_shape=jax.ShapeDtypeStruct((owned, cel...]
    pallas_call x1, Pallas kernels: 27.9 us -> 30 us  [wave(): pl.pallas_call(wave_kernel, out_shape=(jax.ShapeDtypeStruct((B, APX * APZ...]
    unnamed x10 -> x12, local copies, waits for them, and re-layouts: 3.35 us -> 4.01 us
where the time goes in v2:
time: 117 us
  Pallas kernels  110 us (94%)
  local copies, waits for them, and re-layouts  6.46 us (6%)
    pallas_call x1, Pallas kernels, fetch(): pl.pallas_call(fetch_kernel, out_shape=(jax.ShapeDtypeStruct((shots, APX...  40.9 us
    pallas_call x1, Pallas kernels, collect(): pl.pallas_call(collect_kernel, out_shape=jax.ShapeDtypeStruct((owned, cel...  38.6 us
    pallas_call x1, Pallas kernels, wave(): pl.pallas_call(wave_kernel, out_shape=(jax.ShapeDtypeStruct((B, APX * APZ...  30 us
    unnamed x12, local copies, waits for them, and re-layouts  4.01 us

profile of v2, /device:TPU:1, one launch (start us, length us, event | category | flops | bytes accessed | tf_op | source)
XLA Modules:
  0.0 117.1 jit_solution(9573019142439498316)
XLA Ops:
  0.0 0.0 copy-start
  0.7 0.0 copy-start.5
  0.7 0.6 copy-done.5
  1.4 0.1 pad.2.clone
  1.5 0.0 copy-start.4
  1.5 0.7 copy-done.4
  2.1 0.7 gather_fusion
  2.9 0.1 convert_element_type.12
  2.9 0.1 slice.15
  3.0 0.1 rev.7
  3.1 0.1 pad_maximum_fusion.1
  3.2 0.1 tile.7
  3.3 0.1 broadcast_select_fusion.1
  3.3 0.1 select_n.43
  3.4 0.1 select_n.45
  3.5 0.1 maximum_maximum_fusion.names_ref
  3.6 0.0 copy-done
  3.6 0.1 reshape.83
  3.8 0.1 rev.6
  4.0 0.1 pad_maximum_fusion
  4.1 0.2 reshape.84.block_ref
  4.2 40.9 %fetch.1 = (bf16[16,32,512]{2,1,0:T(8,128)(2,1)S(1)}, f32[8,128]{1,0:T(8,128)S(1)}) custom-call(bf16[16,512]{1,0:T(8,128)(2,1)S(1)} %reshape.84.block_ref, f32[8,128]{1,0:T(8,128)S(1)} %maximum_maximum_fusion.names_ref), custom_call_target="tpu_custom_call" | custom-call | flops 300000000 | bytes 2097152 | tf_op jit(solution)/shard_map/fetch/pallas_call | solution.py:490
  45.2 0.0 copy-start.1
  45.2 0.8 copy-done.1
  46.0 30.0 %wave.1 = (s16[16,32,512]{2,1,0:T(8,128)(2,1)}, f32[16,8,128]{2,1,0:T(8,128)}) custom-call(bf16[16,32,512]{2,1,0:T(8,128)(2,1)} %copy-done.1, f32[2,64,16,128]{3,2,1,0:T(8,128)} %bitcast.11, f32[2,64,16,128]{3,2,1,0:T(8,128)} %bitcast.12, s32[1]{0:T(128)S(6)} %copy.12.source_ref, f32[1,8]{1,0:T(1,128)} %pulse_ref.1, s32[1,256]{1,0:T(1,128)} %cells_ref.1, ...), custom_call_target="tpu_custom_call" | custom-call | flops 1000000000 | bytes 5242880 | tf_op jit(solution)/shard_map/wave/pallas_call | solution.py:289
  76.0 0.0 copy-start.2
  76.0 1.0 copy-done.2
  77.0 0.0 copy-start.3
  77.0 0.8 copy-done.3
  77.8 38.6 %collect.1 = f32[16,512]{1,0:T(8,128)S(1)} custom-call(s16[16,32,512]{2,1,0:T(8,128)(2,1)S(1)} %copy-done.2, f32[16,8,128]{2,1,0:T(8,128)S(1)} %copy-done.3, f32[8,128]{1,0:T(8,128)S(1)} %get-tuple-element.12.groups_ref), custom_call_target="tpu_custom_call" | custom-call | flops 500000000 | bytes 2097152 | tf_op jit(solution)/shard_map/collect/pallas_call | solution.py:689
  116.5 0.6 reshape.85
  (8 shorter events, 0.1 us)
Async XLA Ops:
  0.0 3.6 %copy-start = (bf16[16,2,4096]{2,1,0:T(2,128)(2,1)S(1)}, bf16[16,2,4096]{2,1,0:T(2,128)(2,1)}, u32[]{:S(2)}) copy-start(bf16[16,2,4096]{2,1,0:T(2,128)(2,1)} %param.13) | copy-start | bytes 786436
  0.7 0.7 copy-start.5
  1.5 0.7 copy-start.4
  45.2 0.8 copy-start.1
  76.0 1.0 copy-start.2
  77.0 0.8 copy-start.3

commit v3 on v0

v3 whole, which is shorter than its diff:
```python
import jax
import jax.numpy as jnp
import ml_dtypes
import numpy as np
from jax import lax
from jax.experimental import pallas as pl
from jax.experimental.pallas import tpu as pltpu
from jax.sharding import PartitionSpec as P

B = 16
APX = 4
APZ = 8
NX, NY, NZ = 64, 16, 128
STEPS = 8
NREC = 256
COEF_SECOND = (-205.0 / 72.0, 8.0 / 5.0, -1.0 / 5.0, 8.0 / 315.0, -1.0 / 560.0)
COEF_FIRST = (4.0 / 5.0, -1.0 / 5.0, 4.0 / 105.0, -1.0 / 280.0)
SPEED_SCALE = 0.12
F32 = jnp.float32
BF16 = jnp.bfloat16
LEVELS = 32767.0
SMALLEST = 1e-30
MESH = pl.DeviceIdType.MESH
PLANES = 8
CHUNKS = NX // PLANES
ROWS = PLANES * NY
UNROLL = 8
DEPTH_CHIPS = 8
TURNED = tuple((8 - i) % 8 for i in range(8))


def band(extent, centre):
    second = np.zeros((extent, extent))
    first = np.zeros((extent, extent))
    for to in range(extent):
        second[to, to] = centre
        for reach in range(1, 5):
            if to + reach < extent:
                second[to, to + reach] = COEF_SECOND[reach]
                first[to, to + reach] = COEF_FIRST[reach - 1]
            if to - reach >= 0:
                second[to, to - reach] = COEF_SECOND[reach]
                first[to, to - reach] = -COEF_FIRST[reach - 1]
    return second, first


def parts_of(matrix):
    high = matrix.astype(ml_dtypes.bfloat16)
    low = (matrix - high.astype(np.float64)).astype(ml_dtypes.bfloat16)
    return high, low


def depth_matrix():
    second, first = band(NZ, 3.0 * COEF_SECOND[0])
    high, low = parts_of(np.concatenate([second.T, first.T], axis=1))
    return np.concatenate([high, high, low], axis=0)


def middle_matrix():
    second, first = band(NY, 0.0)
    eight = np.eye(PLANES)
    both = np.stack([np.kron(eight, second), np.kron(eight, first)])
    both = both.reshape(2, PLANES * 2, 8, ROWS).transpose(1, 0, 2, 3).reshape(2 * ROWS, ROWS)
    high, low = parts_of(both)
    return np.concatenate([high, high, low], axis=1)


def split_two(values):
    high = values.astype(BF16)
    low = (values - high.astype(F32)).astype(BF16)
    return high, low


def to_levels(values):
    return jnp.round(values).astype(jnp.int32).astype(jnp.int16)


def turn(block, lane_block):
    block = pltpu.roll(block, 0, 1, stride=B, stride_axis=0)
    for bit in (1, 2, 4):
        block = jnp.where((lane_block & bit) != 0, pltpu.roll(block, 8 - bit, 0), block)
    return pltpu.roll(block, 0, 1, stride=B, stride_axis=0)


def products(window_ref, at, depth_ref, middle_ref):
    inner = window_ref[pl.ds(at * PLANES + 4, PLANES)].reshape(ROWS, NZ)
    high, low = split_two(inner)
    along_depth = jnp.dot(
        jnp.concatenate([high, low, high], axis=1), depth_ref[...], preferred_element_type=F32
    )
    along_middle = jnp.dot(
        middle_ref[...], jnp.concatenate([high, low, high], axis=0), preferred_element_type=F32
    )
    return along_depth, along_middle


def each_block(window_ref, at, depth_ref, middle_ref, body):
    along_depth, along_middle = products(window_ref, at, depth_ref, middle_ref)
    base = at * PLANES
    window = [[window_ref[base + j, 8 * half : 8 * half + 8] for half in range(2)] for j in range(8)]
    for plane in range(PLANES):
        window.append([window_ref[base + plane + 8, 8 * half : 8 * half + 8] for half in range(2)])
        for half in range(2):
            row = (plane * 2 + half) * 8
            second = along_depth[row : row + 8, :NZ] + along_middle[2 * row : 2 * row + 8]
            first = None
            for reach in range(1, 5):
                ahead, behind = window[plane + 4 + reach][half], window[plane + 4 - reach][half]
                second = second + COEF_SECOND[reach] * (ahead + behind)
                term = COEF_FIRST[reach - 1] * (ahead - behind)
                first = term if first is None else first + term
            body(
                base + plane, slice(8 * half, 8 * half + 8), window[plane + 4][half],
                second, first, along_middle[2 * row + 8 : 2 * row + 16], along_depth[row : row + 8, NZ:],
            )


def place():
    shot, tile = lax.axis_index("shot"), lax.axis_index("tile")
    shots, depths = lax.axis_size("shot"), DEPTH_CHIPS
    across = lax.axis_size("tile") // depths
    return shot, lax.div(tile, depths), lax.rem(tile, depths), shots, across, depths


def shifted(index, by, size):
    return lax.rem(index + by, size)


def greet(shot, x, z, shots, across, depths):
    barrier = pltpu.get_barrier_semaphore()

    def signal(device_id):
        pl.semaphore_signal(barrier, inc=1, device_id=device_id, device_id_type=MESH)

    def to_shot(by, carry):
        signal((shifted(shot, by, shots), x * depths + z))
        return carry

    lax.fori_loop(1, shots, to_shot, 0)
    for by in range(1, across):
        signal((shot, shifted(x, by, across) * depths + z))
    for by in range(1, depths):
        signal((shot, x * depths + shifted(z, by, depths)))
    pl.semaphore_wait(barrier, shots + across + depths - 3)


def remote(src, dst, send_sem, recv_sem, device_id):
    return pltpu.make_async_remote_copy(
        src_ref=src, dst_ref=dst, send_sem=send_sem, recv_sem=recv_sem,
        device_id=device_id, device_id_type=MESH,
    )


def rows_at(start, size):
    return pl.ds(pl.multiple_of(start, size), size)


def row_levels(values):
    rows, lanes = values.shape
    field = lanes // 2
    units, coded = [], []
    for at in range(2):
        part = values[:, at * field : (at + 1) * field]
        largest = jnp.maximum(jnp.max(jnp.abs(part), axis=1, keepdims=True), SMALLEST)
        units.append(largest * (1.0 / LEVELS))
        coded.append(part * (LEVELS / largest))
    first = lax.broadcasted_iota(jnp.int32, (rows, NZ), 1) == 0
    lines = jnp.transpose(jnp.where(first, units[0], units[1]))[:8]
    return to_levels(jnp.concatenate(coded, axis=1)), lines


def from_levels(levels, units):
    field = levels.shape[1] // 2
    values = levels.astype(F32)
    return jnp.concatenate(
        [values[:, :field] * units[:, 0:1], values[:, field:] * units[:, 1:2]], axis=1
    )


def shot_kernel(
    block_ref, names_ref, source_ref, pulse_ref, cells_ref, traces_ref,
    fwd_hbm, adj_hbm, depth_hbm, middle_hbm,
    out_ref,
    depth_ref, middle_ref, load_sem,
    store_ref, pick_ref, names_all, outgoing, incoming, groups_ref,
    gain_ref, speed_ref, slope_ref, wave_ref, adj_ref, image_ref, first_ref, inject_ref, hot_ref,
    mask_ref, sums_ref,
    grads_ref, units_ref, grads_all, units_all, place_ref, spread_ref,
    whole, whole_levels, whole_lines, from_x, lines_x,
    column, column_levels, column_lines, from_z, lines_z, turned_units,
    z_send, z_recv, x_send, x_recv, name_send, name_recv, shot_send, shot_recv,
    grad_send, grad_recv, unit_send, unit_recv, gx_send, gx_recv, xu_send, xu_recv,
    gz_send, gz_recv, zu_send, zu_recv,
):
    shot, x, z, shots, across, depths = place()
    owned = block_ref.shape[0]
    me = x * depths + z
    positions = APX * APZ
    group = NZ // positions
    total = store_ref.shape[0]
    lane_block = lax.broadcasted_iota(jnp.int32, (8, NZ), 1) // B

    loads = [
        pltpu.make_async_copy(src, dst, load_sem.at[i])
        for i, (src, dst) in enumerate(
            [
                (depth_hbm, depth_ref),
                (middle_hbm, middle_ref),
                (fwd_hbm.at[0, 0], wave_ref.at[0, pl.ds(4, NX)]),
                (fwd_hbm.at[0, 1], wave_ref.at[1, pl.ds(4, NX)]),
                (adj_hbm.at[0, 0], adj_ref.at[0, pl.ds(4, NX)]),
                (adj_hbm.at[0, 1], adj_ref.at[1, pl.ds(4, NX)]),
            ]
        )
    ]
    for load in loads:
        load.start()

    greet(shot, x, z, shots, across, depths)

    store_ref[rows_at(me * owned, owned)] = block_ref[...]
    names_all[shot] = names_ref[...]

    def z_copy(by):
        return remote(
            block_ref, store_ref.at[rows_at(me * owned, owned)], z_send.at[by], z_recv.at[by],
            (shot, x * depths + shifted(z, by, depths)),
        )

    def name_copy(by):
        return remote(
            names_ref, names_all.at[shot], name_send.at[by], name_recv.at[by],
            (shifted(shot, by, shots), me),
        )

    def x_copy(along, by):
        rows = store_ref.at[rows_at((x * depths + shifted(z, depths - by, depths)) * owned, owned)]
        return remote(
            rows, rows, x_send.at[along, by], x_recv.at[along, by],
            (shot, shifted(x, along, across) * depths + z),
        )

    def start_z(by, carry):
        z_copy(by).start()
        return carry

    def start_name(by, carry):
        name_copy(by).start()
        return carry

    def pass_on(by, carry):
        z_copy(by).wait_recv()
        for along in range(1, across):
            x_copy(along, by).start()
        return carry

    lax.fori_loop(1, depths, start_z, 0)
    for along in range(1, across):
        x_copy(along, 0).start()
    lax.fori_loop(1, shots, start_name, 0)
    lax.fori_loop(1, depths, pass_on, 0)

    def wait_name(by, carry):
        name_copy(by).wait_recv()
        return carry

    lax.fori_loop(1, shots, wait_name, 0)

    lines, turned = [], []
    for at in range(8):
        if at < shots // group:
            lines.append(sum(names_all[group * at + i, 0:1] for i in range(group)))
            turned.append(sum(names_all[group * at + i, 1:2] for i in range(group)))
        else:
            lines.append(jnp.zeros((1, NZ), F32))
            turned.append(jnp.zeros((1, NZ), F32))
    groups_ref[...] = jnp.concatenate(turned, axis=0)
    columns = jnp.transpose(jnp.concatenate(lines, axis=0))
    row_ids = lax.broadcasted_iota(jnp.int32, (NZ, total), 1).astype(F32)
    for at in range(shots // group):
        pick_ref[at] = (row_ids == columns[:, at : at + 1]).astype(F32).astype(BF16)

    def wait_x(by, carry):
        for along in range(1, across):
            x_copy(along, by).wait_recv()
        return carry

    lax.fori_loop(0, depths, wait_x, 0)

    def choose(at, carry):
        chosen = jnp.dot(pick_ref[at], store_ref[...], preferred_element_type=F32).astype(BF16)
        outgoing[pl.ds(at * group, group)] = chosen.reshape(group, positions, chosen.shape[1])
        return carry

    lax.fori_loop(0, shots // group, choose, 0)

    def shot_copy(by):
        target = shifted(shot, by, shots)
        return remote(
            outgoing.at[target], incoming.at[shot], shot_send.at[by], shot_recv.at[by], (target, me)
        )

    def start_shot(by, carry):
        shot_copy(by).start()
        return carry

    lax.fori_loop(1, shots, start_shot, 0)
    incoming[shot] = outgoing[shot]

    border = jnp.zeros((4, NY, NZ), F32)
    for ref in (gain_ref, wave_ref.at[0], wave_ref.at[1], adj_ref.at[0], adj_ref.at[1]):
        ref[0:4] = border
        ref[NX + 4 : NX + 8] = border

    source = source_ref[0]
    lane_ids = lax.broadcasted_iota(jnp.int32, (NY, NZ), 1)
    row_of = lax.broadcasted_iota(jnp.int32, (NY, NZ), 0)

    def mark(plane, carry):
        cell = (plane * NY + row_of) * NZ + lane_ids
        mask_ref[plane] = (cell == source).astype(F32)
        return carry

    lax.fori_loop(0, NX, mark, 0)

    cells = cells_ref[...]
    cell_rows = lax.shift_right_logical(cells, 7)
    cell_lanes = jnp.transpose(jnp.broadcast_to((cells & 127).astype(F32), (8, NREC)))[:, 0:1]
    trace_columns = jnp.transpose(traces_ref[...])
    for at in range(8):
        row_ids = lax.broadcasted_iota(jnp.int32, (128, NREC), 0) + at * 128
        hot_ref[at * 128 : at * 128 + 128] = (row_ids == cell_rows).astype(F32).astype(BF16)
    lane_hot = lax.broadcasted_iota(jnp.int32, (NREC, NZ), 1).astype(F32) == cell_lanes
    for step in range(STEPS):
        high, low = split_two(jnp.where(lane_hot, trace_columns[:, step : step + 1], 0.0))
        both = jnp.concatenate([high, low], axis=1)
        added = jnp.dot(hot_ref[...], both, preferred_element_type=F32)
        inject_ref[step] = (added[:, :NZ] + added[:, NZ:]).reshape(NX, NY, NZ)

    store_rows = lax.broadcasted_iota(jnp.int32, (total, NZ), 0).astype(F32)
    for at in range(shots // group):
        hot = (store_rows == groups_ref[at : at + 1]).astype(F32).astype(BF16)
        for part in range(2):
            lanes = (part * (shots // group) + at) * NZ
            place_ref[:, lanes : lanes + NZ] = hot

    def unpack(by, carry):
        plane = shifted(shot, shots - by, shots)
        for block in range(APX):
            at = block * B + plane
            for field in range(2):
                for half in range(2):
                    lanes = (field * 2 + half) * NZ
                    rows_of = incoming[plane, block * 8 : block * 8 + 8, lanes : lanes + NZ].astype(F32)
                    turned = turn(rows_of, lane_block)
                    if field == 0:
                        speed_ref[at, half * 8 : half * 8 + 8] = SPEED_SCALE * turned
                    else:
                        gain_ref[at + 4, half * 8 : half * 8 + 8] = turned
        return carry

    unpack(0, 0)

    def arrived(by, carry):
        shot_copy(by).wait_recv()
        return unpack(by, carry)

    lax.fori_loop(1, shots, arrived, 0)

    for load in loads:
        load.wait()

    def run(window_ref, body):
        def chunk(at, carry):
            each_block(window_ref, at, depth_ref, middle_ref, body)
            return carry

        lax.fori_loop(0, CHUNKS, chunk, 0, unroll=UNROLL)

    def slopes(plane, rows, centre, second, *firsts):
        for axis in range(3):
            slope_ref[axis, plane, rows] = firsts[axis]

    run(gain_ref, slopes)

    def apply(plane, rows, second, firsts):
        applied = gain_ref[plane + 4, rows] * second
        for axis in range(3):
            applied = applied + slope_ref[axis, plane, rows] * firsts[axis]
        return applied

    def forward(step, now_ref, other_ref):
        pulse = pulse_ref[0, step]

        def body(plane, rows, centre, second, *firsts):
            applied = apply(plane, rows, second, firsts)
            image_ref[step, plane, rows] = applied
            for axis in range(3):
                first_ref[step, axis, plane, rows] = firsts[axis]
            newer = 2.0 * centre - other_ref[plane + 4, rows] + speed_ref[plane, rows] * applied
            other_ref[plane + 4, rows] = newer + pulse * mask_ref[plane, rows]

        run(now_ref, body)

    def forward_pair(pair, carry):
        forward(2 * pair, wave_ref.at[1], wave_ref.at[0])
        forward(2 * pair + 1, wave_ref.at[0], wave_ref.at[1])
        return carry

    lax.fori_loop(0, STEPS // 2, forward_pair, 0)

    def backward(step, now_ref, other_ref, start):
        def body(plane, rows, centre, second, *firsts):
            applied = apply(plane, rows, second, firsts)
            newer = 2.0 * centre - other_ref[plane + 4, rows] + speed_ref[plane, rows] * applied
            newer = newer + inject_ref[step, plane, rows]
            other_ref[plane + 4, rows] = newer
            part = newer * image_ref[step, plane, rows]
            if start:
                sums_ref[0, plane, rows] = part
            else:
                sums_ref[0, plane, rows] = sums_ref[0, plane, rows] + part
                part = firsts[0] * first_ref[step + 1, 0, plane, rows]
                part = part + firsts[1] * first_ref[step + 1, 1, plane, rows]
                part = part + firsts[2] * first_ref[step + 1, 2, plane, rows]
                sums_ref[1, plane, rows] = sums_ref[1, plane, rows] + part

        run(now_ref, body)

    def clear(plane, carry):
        sums_ref[1, plane] = jnp.zeros((NY, NZ), F32)
        return carry

    lax.fori_loop(0, NX, clear, 0)
    backward(STEPS - 1, adj_ref.at[1], adj_ref.at[0], True)

    def backward_pair(pair, carry):
        backward(STEPS - 2 - 2 * pair, adj_ref.at[0], adj_ref.at[1], False)
        backward(STEPS - 3 - 2 * pair, adj_ref.at[1], adj_ref.at[0], False)
        return carry

    lax.fori_loop(0, STEPS // 2 - 1, backward_pair, 0)
    backward(0, adj_ref.at[0], adj_ref.at[1], False)

    def last(plane, rows, centre, second, *firsts):
        part = sums_ref[1, plane, rows]
        for axis in range(3):
            part = part + firsts[axis] * first_ref[0, axis, plane, rows]
        sums_ref[1, plane, rows] = part * speed_ref[plane, rows]

    run(adj_ref.at[1], last)

    def code(plane):
        for block in range(APX):
            at = block * B + plane
            for field in range(2):
                values = sums_ref[field, at]
                largest = jnp.max(jnp.abs(values), axis=(0, 1), keepdims=True)
                largest = jnp.maximum(largest, SMALLEST)
                line = field * APX + block
                units_ref[plane, line : line + 1] = jnp.broadcast_to(largest * (1.0 / LEVELS), (1, NZ))
                grads_ref[plane, field, block] = to_levels(values * (LEVELS / largest))

    def grad_copy(by):
        target = shifted(shot, by, shots)
        return remote(
            grads_ref.at[target], grads_all.at[shot], grad_send.at[by], grad_recv.at[by], (target, me)
        )

    def unit_copy(by):
        target = shifted(shot, by, shots)
        return remote(
            units_ref.at[target], units_all.at[shot], unit_send.at[by], unit_recv.at[by], (target, me)
        )

    def start_grad(by, carry):
        code(shifted(shot, by, shots))
        grad_copy(by).start()
        unit_copy(by).start()
        return carry

    lax.fori_loop(1, shots, start_grad, 0)
    code(shot)
    grads_all[shot] = grads_ref[shot]
    units_all[shot] = units_ref[shot]

    def spread(by, carry):
        sender = shifted(shot, shots - by, shots)
        for pair in range(APX // 2):
            for field in range(2):
                halves = [[], []]
                for block in (2 * pair, 2 * pair + 1):
                    line = field * APX + block
                    values = grads_all[sender, field, block].astype(F32) * units_all[sender, line : line + 1]
                    for half in range(2):
                        halves[half].append(turn(values[8 * half : 8 * half + 8], lane_block))
                for half in range(2):
                    lanes = (field * 2 + half) * NZ
                    high, low = split_two(jnp.concatenate(halves[half], axis=0))
                    rows = pl.ds(pl.multiple_of(sender * positions + pair * 16, 16), 16)
                    spread_ref[0, rows, lanes : lanes + NZ] = high
                    spread_ref[1, rows, lanes : lanes + NZ] = low
        return carry

    spread(0, 0)

    def returned(by, carry):
        grad_copy(by).wait_recv()
        unit_copy(by).wait_recv()
        return spread(by, carry)

    lax.fori_loop(1, shots, returned, 0)

    block = depths * owned
    parts = spread_ref[...].reshape(2 * shots * positions, spread_ref.shape[2])
    for at in range(across):
        rows = slice(at * block, at * block + block)
        added = jnp.dot(place_ref[rows], parts, preferred_element_type=F32)
        whole[rows] = added
        coded, units = row_levels(added)
        whole_levels[rows] = coded
        whole_lines[at] = units

    def gx_copy(along):
        target = shifted(x, along, across)
        return remote(
            whole_levels.at[rows_at(target * block, block)], from_x.at[along],
            gx_send.at[along], gx_recv.at[along], (shot, target * depths + z),
        )

    def gx_lines(along):
        target = shifted(x, along, across)
        return remote(
            whole_lines.at[target], lines_x.at[along],
            xu_send.at[along], xu_recv.at[along], (shot, target * depths + z),
        )

    for along in range(1, across):
        gx_copy(along).start()
        gx_lines(along).start()
    summed = whole[rows_at(x * block, block)]
    for along in range(1, across):
        gx_copy(along).wait_recv()
        gx_lines(along).wait_recv()
        summed = summed + from_levels(from_x[along], jnp.transpose(lines_x[along]))
    column[...] = summed
    coded, units = row_levels(summed)
    column_levels[...] = coded
    column_lines[...] = units

    def gz_copy(by):
        target = shifted(z, by, depths)
        return remote(
            column_levels.at[rows_at(target * owned, owned)], from_z.at[by],
            gz_send.at[by], gz_recv.at[by], (shot, x * depths + target),
        )

    def gz_lines(by):
        target = shifted(z, by, depths)
        return remote(
            column_lines, lines_z.at[by], zu_send.at[by], zu_recv.at[by], (shot, x * depths + target)
        )

    for by in range(1, depths):
        gz_copy(by).start()
        gz_lines(by).start()
    mine = column[rows_at(z * owned, owned)]
    for by in range(1, depths):
        gz_copy(by).wait_recv()
        gz_lines(by).wait_recv()
        turned_units[by] = jnp.transpose(lines_z[by])
        mine = mine + from_levels(from_z[by], turned_units[by, rows_at(z * owned, owned)])
    out_ref[...] = mine

    def finish_shots(by, carry):
        shot_copy(by).wait_send()
        name_copy(by).wait_send()
        grad_copy(by).wait_send()
        unit_copy(by).wait_send()
        return carry

    def finish_z(by, carry):
        z_copy(by).wait_send()
        gz_copy(by).wait_send()
        gz_lines(by).wait_send()
        return carry

    def finish_x(by, carry):
        for along in range(1, across):
            x_copy(along, by).wait_send()
        return carry

    lax.fori_loop(1, shots, finish_shots, 0)
    lax.fori_loop(1, depths, finish_z, 0)
    lax.fori_loop(0, depths, finish_x, 0)
    for along in range(1, across):
        gx_copy(along).wait_send()
        gx_lines(along).wait_send()


def shot_gradients(block, names, source, pulses, cells, traces, fwd, adj, shots, tiles):
    vmem = pl.BlockSpec(memory_space=pltpu.VMEM)
    smem = pl.BlockSpec(memory_space=pltpu.SMEM)
    hbm = pl.BlockSpec(memory_space=pl.ANY)
    owned, lanes = block.shape
    depths = DEPTH_CHIPS
    across = tiles // depths
    total = tiles * owned
    positions = APX * APZ
    groups = shots * positions // NZ
    rows = depths * owned
    volume = (NX, NY, NZ)
    padded = (NX + 8, NY, NZ)
    int16 = jnp.int16
    dma = pltpu.SemaphoreType.DMA
    depth, middle = depth_matrix(), middle_matrix()
    return pl.pallas_call(
        shot_kernel,
        out_shape=jax.ShapeDtypeStruct((owned, lanes), F32),
        in_specs=[vmem, vmem, smem, smem, vmem, vmem, hbm, hbm, hbm, hbm],
        out_specs=vmem,
        scratch_shapes=[
            pltpu.VMEM(depth.shape, BF16),
            pltpu.VMEM(middle.shape, BF16),
            dma((6,)),
            pltpu.VMEM((total, lanes), BF16),
            pltpu.VMEM((groups, NZ, total), BF16),
            pltpu.VMEM((shots, 8, NZ), F32),
            pltpu.VMEM((shots, positions, lanes), BF16),
            pltpu.VMEM((shots, positions, lanes), BF16),
            pltpu.VMEM((8, NZ), F32),
            pltpu.VMEM(padded, F32),
            pltpu.VMEM(volume, F32),
            pltpu.VMEM((3,) + volume, F32),
            pltpu.VMEM((2,) + padded, F32),
            pltpu.VMEM((2,) + padded, F32),
            pltpu.VMEM((STEPS,) + volume, F32),
            pltpu.VMEM((STEPS, 3) + volume, F32),
            pltpu.VMEM((STEPS,) + volume, F32),
            pltpu.VMEM((NX * NY, NREC), BF16),
            pltpu.VMEM(volume, F32),
            pltpu.VMEM((2,) + volume, F32),
            pltpu.VMEM((B, 2, APX, NY, NZ), int16),
            pltpu.VMEM((B, 8, NZ), F32),
            pltpu.VMEM((shots, 2, APX, NY, NZ), int16),
            pltpu.VMEM((shots, 8, NZ), F32),
            pltpu.VMEM((total, 2 * groups * NZ), BF16),
            pltpu.VMEM((2, shots * positions, lanes), BF16),
            pltpu.VMEM((total, lanes), F32),
            pltpu.VMEM((total, lanes), int16),
            pltpu.VMEM((across, 8, rows), F32),
            pltpu.VMEM((across, rows, lanes), int16),
            pltpu.VMEM((across, 8, rows), F32),
            pltpu.VMEM((rows, lanes), F32),
            pltpu.VMEM((rows, lanes), int16),
            pltpu.VMEM((8, rows), F32),
            pltpu.VMEM((depths, owned, lanes), int16),
            pltpu.VMEM((depths, 8, rows), F32),
            pltpu.VMEM((depths, rows, 8), F32),
            dma((depths,)), dma((depths,)),
            dma((across, depths)), dma((across, depths)),
            dma((shots,)), dma((shots,)), dma((shots,)), dma((shots,)),
            dma((shots,)), dma((shots,)), dma((shots,)), dma((shots,)),
            dma((across,)), dma((across,)), dma((across,)), dma((across,)),
            dma((depths,)), dma((depths,)), dma((depths,)), dma((depths,)),
        ],
        compiler_params=pltpu.CompilerParams(
            collective_id=0, has_side_effects=True, vmem_limit_bytes=56 * 1024 * 1024
        ),
        cost_estimate=pl.CostEstimate(flops=2 * 10**9, bytes_accessed=5 * 2**20, transcendentals=0),
        name="shot_gradients",
    )(block, names, source, pulses, cells, traces, fwd, adj, jnp.asarray(depth), jnp.asarray(middle))


def per_device(
    tile_store, apertures, model, fwd_states, adj_states, source_cell, wavelet, receiver_cells, residuals
):
    shot = lax.axis_index("shot")
    shots, tiles = lax.axis_size("shot"), lax.axis_size("tile")
    owned = model.shape[0]
    positions = APX * APZ
    cells = model.shape[2] // shots

    rows = tile_store[apertures[0]].astype(F32)
    turned = rows.reshape(APX, APZ)
    turned = jnp.concatenate([turned[:, :1], turned[:, :0:-1]], axis=1).reshape(positions)
    group = NZ // positions
    mine = jnp.repeat(jnp.arange(group) == lax.rem(shot, group), positions)
    lines = [jnp.where(mine, jnp.tile(line, group), 0.0) for line in (rows, turned)]
    names = jnp.concatenate([jnp.stack(lines), jnp.zeros((6, NZ), F32)])

    block = lax.dynamic_slice_in_dim(model, shot * cells, cells, axis=2)
    block = block.reshape(owned, 4, 8, B)
    block = jnp.concatenate([block[:, :, :1], block[:, :, :0:-1]], axis=2).reshape(owned, 2 * cells)

    sums = shot_gradients(
        block, names, source_cell, wavelet, receiver_cells, residuals[0], fwd_states, adj_states,
        shots, tiles,
    )
    return sums.reshape(owned, 2, cells)


def solution(mesh):
    return jax.shard_map(
        per_device,
        mesh=mesh,
        in_specs=(
            P(),
            P(("shot", "tile"), None),
            P("tile", None, None),
            P(("shot", "tile"), None, None, None, None),
            P(("shot", "tile"), None, None, None, None),
            P(("shot", "tile")),
            P(("shot", "tile"), None),
            P(("shot", "tile"), None),
            P(("shot", "tile"), None, None),
        ),
        out_specs=P("tile", None, "shot"),
        check_vma=False,
    )
```

time: 552 us -> 105 us (0.19)
  other arithmetic: 212 us -> 0.93 us
  waiting for transfers between devices: 196 us -> 0 us
  local copies, waits for them, and re-layouts: 105 us -> 5.15 us
  Pallas kernels: 0 us -> 97.7 us
  starting transfers between devices: 18.9 us -> 0 us
  between operations: 14.3 us -> 0.77 us
    add x28 -> x0, other arithmetic: 159 us -> none  [the longest x8 86.2 us: adjoint_step(): grad_gain = grad_gain + speed * product]
    pallas_call x0 -> x1, Pallas kernels: none -> 97.7 us  [shot_gradients(): pl.pallas_call(shot_kernel, out_shape=jax.ShapeDtypeStruct((owned, lanes)...]
    all_gather x1 -> x0, waiting for transfers between devices: 91.6 us -> none  [per_device(): shard_rows = lax.all_gather(model, 'tile', axis=0, tiled=True)]
    reduce_scatter x1 -> x0, waiting for transfers between devices: 56.3 us -> none  [per_device(): return lax.psum_scatter(owned_sum, 'shot', scatter_dimension=2, tiled=True)]
    all_to_all x2 -> x0, waiting for transfers between devices: 47.3 us -> none  [the longest x1 47.3 us: per_device(): lax.all_to_all(outgoing, 'tile', split_axis=0, concat_axis=0, tiled=True)]
    dynamic_update_slice x8 -> x0, other arithmetic: 22.8 us -> none  [evolve(): lax.scan(forward_step, (fwd_pair[0], fwd_pair[1]), pulses)]
    squeeze x11 -> x0, local copies, waits for them, and re-layouts: 22.5 us -> none  [the longest x8 15 us: evolve(): lax.scan(adjoint_step, (adj_pair[0], adj_pair[1], zeros_field, zeros_fiel...]
    while x64 -> x0, local copies, waits for them, and re-layouts: 19.6 us -> none
  transfers between devices with their start and end apart: 4 -> 0, of which waited for: 3 -> 0; matrix products, arithmetic and copies ran while one was open for 57% -> 0% of each run, Pallas kernels for 0% -> 0%
where the time goes in v3:
time: 105 us
  Pallas kernels  97.7 us (93%)
  local copies, waits for them, and re-layouts  5.15 us (5%)
    pallas_call x1, Pallas kernels, shot_gradients(): pl.pallas_call(shot_kernel, out_shape=jax.ShapeDtypeStruct((owned, lanes)...  97.7 us

profile of v3, /device:TPU:1, one launch (start us, length us, event | category | flops | bytes accessed | tf_op | source)
XLA Modules:
  0.0 104.5 jit_solution(3223109751044156218)
XLA Ops:
  0.0 0.0 copy-start
  0.7 0.0 copy-start.2
  0.7 0.6 copy-done.2
  1.4 0.1 pad.2.clone
  1.5 0.0 copy-start.1
  1.5 0.7 copy-done.1
  2.1 0.7 gather_fusion
  2.9 0.1 convert_element_type.12
  2.9 0.1 slice.15
  3.0 0.1 rev.7
  3.1 0.1 pad_maximum_fusion.1
  3.2 0.1 tile.7
  3.3 0.1 broadcast_select_fusion.1
  3.3 0.1 select_n.43
  3.4 0.1 select_n.45
  3.5 0.7 maximum_maximum_fusion.names_ref
  4.2 0.0 copy-done
  4.2 0.1 reshape.83
  4.4 0.1 rev.6
  4.6 0.1 pad_maximum_fusion
  4.7 0.8 reshape.84.block_ref
  5.4 97.7 %shot_gradients.1 = f32[16,512]{1,0:T(8,128)} custom-call(bf16[16,512]{1,0:T(8,128)(2,1)} %reshape.84.block_ref, f32[8,128]{1,0:T(8,128)} %maximum_maximum_fusion.names_ref, s32[1]{0:T(128)S(6)} %copy.12.source_ref, f32[1,8]{1,0:T(1,128)} %pulse_ref.1, s32[1,256]{1,0:T(1,128)} %cells_ref.1, f32[8,256]{1,0:T(8,128)} %bitcast.9, ...), custom_call_target="tpu_custom_call" | custom-call | flops 2000000000 | bytes 5242880 | tf_op jit(solution)/shard_map/shot_gradients/pallas_call | solution.py:617
  103.1 1.4 %reshape.85 = f32[16,2,256]{2,1,0:T(2,128)} reshape(f32[16,512]{1,0:T(8,128)} %shot_gradients.1) | data formatting | bytes 65536 | tf_op jit(solution)/shard_map/reshape | solution.py:700
  (8 shorter events, 0.1 us)
Async XLA Ops:
  0.0 4.2 %copy-start = (bf16[16,2,4096]{2,1,0:T(2,128)(2,1)S(1)}, bf16[16,2,4096]{2,1,0:T(2,128)(2,1)}, u32[]{:S(2)}) copy-start(bf16[16,2,4096]{2,1,0:T(2,128)(2,1)} %param.13) | copy-start | bytes 786436
  0.7 0.7 copy-start.2
  1.5 0.7 copy-start.1

commit v4 on v3

v4 whole, which is shorter than its diff:
```python
import jax
import jax.numpy as jnp
import ml_dtypes
import numpy as np
from jax import lax
from jax.experimental import pallas as pl
from jax.experimental.pallas import tpu as pltpu
from jax.sharding import PartitionSpec as P

B = 16
APX = 4
APZ = 8
NX, NY, NZ = 64, 16, 128
STEPS = 8
NREC = 256
COEF_SECOND = (-205.0 / 72.0, 8.0 / 5.0, -1.0 / 5.0, 8.0 / 315.0, -1.0 / 560.0)
COEF_FIRST = (4.0 / 5.0, -1.0 / 5.0, 4.0 / 105.0, -1.0 / 280.0)
SPEED_SCALE = 0.12
F32 = jnp.float32
BF16 = jnp.bfloat16
LEVELS = 32767.0
SMALLEST = 1e-30
MESH = pl.DeviceIdType.MESH
PLANES = 8
CHUNKS = NX // PLANES
ROWS = PLANES * NY
UNROLL = 8
DEPTH_CHIPS = 8
TURNED = tuple((8 - i) % 8 for i in range(8))


def band(extent, centre):
    second = np.zeros((extent, extent))
    first = np.zeros((extent, extent))
    for to in range(extent):
        second[to, to] = centre
        for reach in range(1, 5):
            if to + reach < extent:
                second[to, to + reach] = COEF_SECOND[reach]
                first[to, to + reach] = COEF_FIRST[reach - 1]
            if to - reach >= 0:
                second[to, to - reach] = COEF_SECOND[reach]
                first[to, to - reach] = -COEF_FIRST[reach - 1]
    return second, first


def parts_of(matrix):
    high = matrix.astype(ml_dtypes.bfloat16)
    low = (matrix - high.astype(np.float64)).astype(ml_dtypes.bfloat16)
    return high, low


def depth_matrix():
    second, first = band(NZ, 3.0 * COEF_SECOND[0])
    high, low = parts_of(np.concatenate([second.T, first.T], axis=1))
    return np.concatenate([high, high, low], axis=0)


def middle_matrix():
    second, first = band(NY, 0.0)
    eight = np.eye(PLANES)
    both = np.stack([np.kron(eight, second), np.kron(eight, first)])
    both = both.reshape(2, PLANES * 2, 8, ROWS).transpose(1, 0, 2, 3).reshape(2 * ROWS, ROWS)
    high, low = parts_of(both)
    return np.concatenate([high, high, low], axis=1)


def split_two(values):
    high = values.astype(BF16)
    low = (values - high.astype(F32)).astype(BF16)
    return high, low


def to_levels(values):
    return jnp.round(values).astype(jnp.int32).astype(jnp.int16)


def turn(block, lane_block):
    block = pltpu.roll(block, 0, 1, stride=B, stride_axis=0)
    for bit in (1, 2, 4):
        block = jnp.where((lane_block & bit) != 0, pltpu.roll(block, 8 - bit, 0), block)
    return pltpu.roll(block, 0, 1, stride=B, stride_axis=0)


def products(window_ref, at, depth_ref, middle_ref):
    inner = window_ref[pl.ds(at * PLANES + 4, PLANES)].reshape(ROWS, NZ)
    high, low = split_two(inner)
    along_depth = jnp.dot(
        jnp.concatenate([high, low, high], axis=1), depth_ref[...], preferred_element_type=F32
    )
    along_middle = jnp.dot(
        middle_ref[...], jnp.concatenate([high, low, high], axis=0), preferred_element_type=F32
    )
    return along_depth, along_middle


def each_block(window_ref, at, depth_ref, middle_ref, body):
    along_depth, along_middle = products(window_ref, at, depth_ref, middle_ref)
    base = at * PLANES
    window = [[window_ref[base + j, 8 * half : 8 * half + 8] for half in range(2)] for j in range(8)]
    for plane in range(PLANES):
        window.append([window_ref[base + plane + 8, 8 * half : 8 * half + 8] for half in range(2)])
        for half in range(2):
            row = (plane * 2 + half) * 8
            second = along_depth[row : row + 8, :NZ] + along_middle[2 * row : 2 * row + 8]
            first = None
            for reach in range(1, 5):
                ahead, behind = window[plane + 4 + reach][half], window[plane + 4 - reach][half]
                second = second + COEF_SECOND[reach] * (ahead + behind)
                term = COEF_FIRST[reach - 1] * (ahead - behind)
                first = term if first is None else first + term
            body(
                base + plane, slice(8 * half, 8 * half + 8), window[plane + 4][half],
                second, first, along_middle[2 * row + 8 : 2 * row + 16], along_depth[row : row + 8, NZ:],
            )


def place():
    shot, tile = lax.axis_index("shot"), lax.axis_index("tile")
    return lax.div(shot, 2), lax.rem(shot, 2), lax.div(tile, DEPTH_CHIPS), lax.rem(tile, DEPTH_CHIPS)


def shifted(index, by, size):
    return lax.rem(index + by, size)


def chunk_of(route, index, y):
    if route == 0:
        return index
    return lax.rem(3 * y + lax.div(index, 2), DEPTH_CHIPS) * 2 + lax.rem(index, 2)


def greet(y, core, x, z, shots, across, depths):
    barrier = pltpu.get_barrier_semaphore()
    shot, turned_shot = y * 2 + core, z * 2 + core

    def signal(device_id):
        pl.semaphore_signal(barrier, inc=1, device_id=device_id, device_id_type=MESH)

    for by in range(1, depths):
        signal((shot, x * depths + shifted(z, by, depths)))
    for by in range(1, across):
        signal((shot, shifted(x, by, across) * depths + z))

    def to_columns(by, carry):
        signal((shifted(shot, by, shots), x * depths + z))
        other = shifted(turned_shot, by, shots)
        signal((y * 2 + lax.rem(other, 2), x * depths + lax.div(other, 2)))
        return carry

    lax.fori_loop(1, shots, to_columns, 0)
    home = lax.rem(3 * y + z, depths)

    def to_last(from_y, carry):
        @pl.when(jnp.logical_or(from_y != y, home != y))
        def _():
            signal((from_y * 2 + core, x * depths + lax.rem(y + 3 * depths - 3 * from_y, depths)))

        return carry

    lax.fori_loop(0, depths, to_last, 0)
    here = jnp.where(home == y, 1, 0)
    return barrier, 2 * (shots - 1) + across - 1 + depths - 1 + depths - here


def remote(src, dst, send_sem, recv_sem, device_id):
    return pltpu.make_async_remote_copy(
        src_ref=src, dst_ref=dst, send_sem=send_sem, recv_sem=recv_sem,
        device_id=device_id, device_id_type=MESH,
    )


def rows_at(start, size):
    return pl.ds(pl.multiple_of(start, size), size)


def row_levels(values):
    rows, lanes = values.shape
    lane = lax.broadcasted_iota(jnp.int32, (rows, NZ), 1)
    coded, units = [], jnp.zeros((rows, NZ), F32)
    for at in range(lanes // NZ):
        part = values[:, at * NZ : (at + 1) * NZ]
        largest = jnp.maximum(jnp.max(jnp.abs(part), axis=1, keepdims=True), SMALLEST)
        units = jnp.where(lane == at, largest * (1.0 / LEVELS), units)
        coded.append(part * (LEVELS / largest))
    return to_levels(jnp.concatenate(coded, axis=1)), jnp.transpose(units)[:8]


def from_levels(levels, units):
    values = levels.astype(F32)
    return jnp.concatenate(
        [values[:, at * NZ : (at + 1) * NZ] * units[:, at : at + 1] for at in range(values.shape[1] // NZ)],
        axis=1,
    )


def shot_kernel(
    tile_store_ref, aperture_ref, model_ref, source_ref, pulse_ref, cells_ref, traces_ref,
    fwd_hbm, adj_hbm, depth_hbm, middle_hbm,
    out_ref,
    depth_ref, middle_ref, depth_f32, middle_f32, load_sem,
    blocks_ref, names_ref, store_ref, pick_ref, names_all, outgoing, incoming,
    gain_ref, speed_ref, slope_ref, wave_ref, adj_ref, image_ref, first_ref, inject_ref, hot_ref,
    mask_ref, sums_ref,
    grads_ref, units_ref, grads_all, units_all, place_ref, spread_ref,
    whole_levels, whole_lines, from_x, lines_x, column, from_z,
    z_send, z_recv, x_send, x_recv, name_send, name_recv, shot_send, shot_recv,
    grad_send, grad_recv, unit_send, unit_recv, gx_send, gx_recv, xu_send, xu_recv,
    gz_send, gz_recv,
):
    y, core, x, z = place()
    shots, across, depths = names_all.shape[1], from_x.shape[1], DEPTH_CHIPS
    owned = model_ref.shape[0]
    me = x * depths + z
    positions = APX * APZ
    group = NZ // positions
    total = store_ref.shape[0] * owned
    cells_of = model_ref.shape[1] // 2
    lane_block = lax.broadcasted_iota(jnp.int32, (8, NZ), 1) // B

    mine = (y * 2 + core, z * 2 + core)

    def on_route(route, index):
        if route == 0:
            return (index, me)
        return (y * 2 + lax.rem(index, 2), x * depths + lax.div(index, 2))

    loads = [
        pltpu.make_async_copy(src, dst, load_sem.at[i])
        for i, (src, dst) in enumerate(
            [
                (depth_hbm, depth_f32),
                (middle_hbm, middle_f32),
                (fwd_hbm.at[0, 0], wave_ref.at[0, pl.ds(4, NX)]),
                (fwd_hbm.at[0, 1], wave_ref.at[1, pl.ds(4, NX)]),
                (adj_hbm.at[0, 0], adj_ref.at[0, pl.ds(4, NX)]),
                (adj_hbm.at[0, 1], adj_ref.at[1, pl.ds(4, NX)]),
            ]
        )
    ]
    barrier, greeted = greet(y, core, x, z, shots, across, depths)
    for load in loads:
        load.start()

    from_lane = lax.broadcasted_iota(jnp.int32, (NZ, NZ), 0)
    to_lane = lax.broadcasted_iota(jnp.int32, (NZ, NZ), 1)
    mirror = (from_lane % B == to_lane % B) & (from_lane // B == (8 - to_lane // B) % 8)
    mirror = mirror.astype(F32).astype(BF16)

    def cut(chunk, route):
        parts = []
        for field in range(2):
            start = pl.multiple_of(field * cells_of + chunk * 2 * NZ + route * NZ, NZ)
            parts.append(model_ref[:, pl.ds(start, NZ)])
        return jnp.concatenate(parts, axis=0)

    cuts = [cut(mine[0], 0)] + [
        cut(chunk_of(1, to * 2 + core, y), 1) for to in range(depths)
    ]
    mirrored = jnp.dot(jnp.concatenate(cuts, axis=0), mirror, preferred_element_type=F32).astype(BF16)
    for to in range(depths):
        for route in range(2):
            for field in range(2):
                row = ((route * (to + 1)) * 2 + field) * owned
                blocks_ref[to, route, :, field * NZ : field * NZ + NZ] = mirrored[row : row + owned]

    wanted = jnp.concatenate([aperture_ref[...]] * group, axis=1)
    tile_ids = lax.broadcasted_iota(jnp.int32, (total, NZ), 0)
    chosen = (tile_ids == wanted).astype(F32).astype(BF16)
    digits = jnp.broadcast_to(tile_store_ref[...], (8, total))
    digit_row = lax.broadcasted_iota(jnp.int32, (8, total), 0)
    digits = jnp.where(digit_row == 0, lax.shift_right_logical(digits, 4), digits & 15)
    found = jnp.dot(digits.astype(F32).astype(BF16), chosen, preferred_element_type=F32)
    turn_lanes = (from_lane // 8 == to_lane // 8) & (from_lane % 8 == (8 - to_lane % 8) % 8)
    found_turned = jnp.dot(
        found.astype(BF16), turn_lanes.astype(F32).astype(BF16), preferred_element_type=F32
    )
    lane_group = lax.broadcasted_iota(jnp.int32, (1, NZ), 1) // positions
    for route in range(2):
        member = lane_group == lax.rem(mine[route], group)
        for kind, digits_of in enumerate((found, found_turned)):
            line = 16.0 * digits_of[0:1] + digits_of[1:2]
            names_ref[2 * route + kind : 2 * route + kind + 1] = jnp.where(member, line, 0.0)

    pl.semaphore_wait(barrier, greeted)

    store_ref[me] = blocks_ref[z]
    for route in range(2):
        names_all[route, mine[route]] = names_ref[...]

    def z_copy(by):
        target = shifted(z, by, depths)
        return remote(
            blocks_ref.at[target], store_ref.at[me],
            z_send.at[by], z_recv.at[by], (mine[0], x * depths + target),
        )

    def name_copy(route, by):
        return remote(
            names_ref, names_all.at[route, mine[route]],
            name_send.at[route, by], name_recv.at[route, by],
            on_route(route, shifted(mine[route], by, shots)),
        )

    def x_copy(route, along):
        part = store_ref.at[pl.ds(x * depths, depths), route]
        return remote(
            part, part, x_send.at[route, along], x_recv.at[route, along],
            (mine[0], shifted(x, along, across) * depths + z),
        )

    def start_z(by, carry):
        z_copy(by).start()
        return carry

    def start_name(by, carry):
        for route in range(2):
            name_copy(route, by).start()
        return carry

    def wait_z(by, carry):
        z_copy(by).wait_recv()
        return carry

    lax.fori_loop(1, depths, start_z, 0)
    lax.fori_loop(1, shots, start_name, 0)
    lax.fori_loop(1, depths, wait_z, 0)
    for route in range(2):
        for along in (2, 1, 3):
            x_copy(route, along).start()

    def wait_name(by, carry):
        for route in range(2):
            name_copy(route, by).wait_recv()
        return carry

    lax.fori_loop(1, shots, wait_name, 0)

    groups = shots // group
    lines = [
        sum(names_all[route, group * at + i, 2 * route : 2 * route + 1] for i in range(group))
        for route in range(2)
        for at in range(groups)
    ]
    columns = jnp.transpose(jnp.concatenate(lines, axis=0))
    row_ids = lax.broadcasted_iota(jnp.int32, (NZ, total), 1).astype(F32)
    for route in range(2):
        for at in range(groups):
            column_at = route * groups + at
            hot = (row_ids == columns[:, column_at : column_at + 1]).astype(F32).astype(BF16)
            pick_ref[route, at * NZ : at * NZ + NZ] = hot

    def shot_copy(route, by):
        target = shifted(mine[route], by, shots)
        return remote(
            outgoing.at[route, target], incoming.at[route, mine[route]],
            shot_send.at[route, by], shot_recv.at[route, by], on_route(route, target),
        )

    for route in range(2):
        for along in (1, 3, 2):
            x_copy(route, along).wait_recv()
        held = store_ref[:, route].reshape(total, 2 * NZ)
        picked = jnp.dot(pick_ref[route], held, preferred_element_type=F32)
        outgoing[route] = picked.astype(BF16).reshape(shots, positions, 2 * NZ)

        def start_shot(by, carry):
            shot_copy(route, by).start()
            return carry

        lax.fori_loop(1, shots, start_shot, 0)
    for route in range(2):
        incoming[route, mine[route]] = outgoing[route, mine[route]]

    for load in loads:
        load.wait()
    depth_ref[...] = depth_f32[...].astype(BF16)
    middle_ref[...] = middle_f32[...].astype(BF16)
    border = jnp.zeros((4, NY, NZ), F32)
    for ref in (gain_ref, wave_ref.at[0], wave_ref.at[1], adj_ref.at[0], adj_ref.at[1]):
        ref[0:4] = border
        ref[NX + 4 : NX + 8] = border

    source = source_ref[0]
    lane_ids = lax.broadcasted_iota(jnp.int32, (NY, NZ), 1)
    row_of = lax.broadcasted_iota(jnp.int32, (NY, NZ), 0)

    def mark(plane, carry):
        cell = (plane * NY + row_of) * NZ + lane_ids
        mask_ref[plane] = (cell == source).astype(F32)
        sums_ref[1, plane] = jnp.zeros((NY, NZ), F32)
        return carry

    lax.fori_loop(0, NX, mark, 0)

    cells = cells_ref[...]
    cell_rows = lax.shift_right_logical(cells, 7)
    cell_lanes = jnp.transpose(jnp.broadcast_to((cells & 127).astype(F32), (8, NREC)))[:, 0:1]
    trace_columns = jnp.transpose(traces_ref[...])
    for at in range(8):
        row_ids = lax.broadcasted_iota(jnp.int32, (128, NREC), 0) + at * 128
        hot_ref[at * 128 : at * 128 + 128] = (row_ids == cell_rows).astype(F32).astype(BF16)
    lane_hot = lax.broadcasted_iota(jnp.int32, (NREC, NZ), 1).astype(F32) == cell_lanes
    for step in range(STEPS):
        high, low = split_two(jnp.where(lane_hot, trace_columns[:, step : step + 1], 0.0))
        both = jnp.concatenate([high, low], axis=1)
        added = jnp.dot(hot_ref[...], both, preferred_element_type=F32)
        inject_ref[step] = (added[:, :NZ] + added[:, NZ:]).reshape(NX, NY, NZ)

    store_rows = lax.broadcasted_iota(jnp.int32, (total, NZ), 0).astype(F32)
    for route in range(2):
        for at in range(groups):
            line = sum(names_all[route, group * at + i, 2 * route + 1 : 2 * route + 2] for i in range(group))
            hot = (store_rows == line).astype(F32).astype(BF16)
            for part in range(2):
                lanes = (part * groups + at) * NZ
                place_ref[route, :, lanes : lanes + NZ] = hot

    def unpack(route, by):
        sender = shifted(mine[route], shots - by, shots)
        plane = chunk_of(route, sender, y)
        for block in range(APX):
            at = block * B + plane
            for field in range(2):
                part = incoming[route, sender, block * 8 : block * 8 + 8, field * NZ : field * NZ + NZ]
                turned = turn(part.astype(F32), lane_block)
                if field == 0:
                    speed_ref[at, 8 * route : 8 * route + 8] = SPEED_SCALE * turned
                else:
                    gain_ref[at + 4, 8 * route : 8 * route + 8] = turned

    def arrived(by, carry):
        for route in range(2):
            shot_copy(route, by).wait_recv()
            unpack(route, by)
        return carry

    for route in range(2):
        unpack(route, 0)
    lax.fori_loop(1, shots, arrived, 0)

    def run(window_ref, body):
        def chunk(at, carry):
            each_block(window_ref, at, depth_ref, middle_ref, body)
            return carry

        lax.fori_loop(0, CHUNKS, chunk, 0, unroll=UNROLL)

    def slopes(plane, rows, centre, second, *firsts):
        for axis in range(3):
            slope_ref[axis, plane, rows] = firsts[axis]

    run(gain_ref, slopes)

    def apply(plane, rows, second, firsts):
        applied = gain_ref[plane + 4, rows] * second
        for axis in range(3):
            applied = applied + slope_ref[axis, plane, rows] * firsts[axis]
        return applied

    def forward(step, now_ref, other_ref):
        pulse = pulse_ref[0, step]

        def body(plane, rows, centre, second, *firsts):
            applied = apply(plane, rows, second, firsts)
            image_ref[step, plane, rows] = applied
            for axis in range(3):
                first_ref[step, axis, plane, rows] = firsts[axis]
            newer = 2.0 * centre - other_ref[plane + 4, rows] + speed_ref[plane, rows] * applied
            other_ref[plane + 4, rows] = newer + pulse * mask_ref[plane, rows]

        run(now_ref, body)

    def forward_pair(pair, carry):
        forward(2 * pair, wave_ref.at[1], wave_ref.at[0])
        forward(2 * pair + 1, wave_ref.at[0], wave_ref.at[1])
        return carry

    lax.fori_loop(0, STEPS // 2, forward_pair, 0)

    def backward(step, now_ref, other_ref, start):
        def body(plane, rows, centre, second, *firsts):
            applied = apply(plane, rows, second, firsts)
            newer = 2.0 * centre - other_ref[plane + 4, rows] + speed_ref[plane, rows] * applied
            newer = newer + inject_ref[step, plane, rows]
            other_ref[plane + 4, rows] = newer
            part = newer * image_ref[step, plane, rows]
            if start:
                sums_ref[0, plane, rows] = part
            else:
                sums_ref[0, plane, rows] = sums_ref[0, plane, rows] + part
                part = firsts[0] * first_ref[step + 1, 0, plane, rows]
                part = part + firsts[1] * first_ref[step + 1, 1, plane, rows]
                part = part + firsts[2] * first_ref[step + 1, 2, plane, rows]
                sums_ref[1, plane, rows] = sums_ref[1, plane, rows] + part

        run(now_ref, body)

    backward(STEPS - 1, adj_ref.at[1], adj_ref.at[0], True)

    def backward_pair(pair, carry):
        backward(STEPS - 2 - 2 * pair, adj_ref.at[0], adj_ref.at[1], False)
        backward(STEPS - 3 - 2 * pair, adj_ref.at[1], adj_ref.at[0], False)
        return carry

    lax.fori_loop(0, STEPS // 2 - 1, backward_pair, 0)
    backward(0, adj_ref.at[0], adj_ref.at[1], False)

    def last(plane, rows, centre, second, *firsts):
        part = sums_ref[1, plane, rows]
        for axis in range(3):
            part = part + firsts[axis] * first_ref[0, axis, plane, rows]
        sums_ref[1, plane, rows] = part * speed_ref[plane, rows]

    run(adj_ref.at[1], last)

    def code(route, index):
        plane = chunk_of(route, index, y)
        for field in range(2):
            values = [
                sums_ref[field, block * B + plane, 8 * route : 8 * route + 8] for block in range(APX)
            ]
            largest = jnp.abs(values[0])
            for value in values[1:]:
                largest = jnp.maximum(largest, jnp.abs(value))
            largest = jnp.maximum(jnp.max(largest, axis=(0, 1), keepdims=True), SMALLEST)
            units_ref[route, index, field : field + 1] = jnp.broadcast_to(largest * (1.0 / LEVELS), (1, NZ))
            levels = LEVELS / largest
            for pair in range(APX // 2):
                both = jnp.concatenate(values[2 * pair : 2 * pair + 2], axis=0)
                grads_ref[route, index, field, pair] = to_levels(both * levels)

    def grad_copy(route, by):
        target = shifted(mine[route], by, shots)
        return remote(
            grads_ref.at[route, target], grads_all.at[route, mine[route]],
            grad_send.at[route, by], grad_recv.at[route, by], on_route(route, target),
        )

    def unit_copy(route, by):
        target = shifted(mine[route], by, shots)
        return remote(
            units_ref.at[route, target], units_all.at[route, mine[route]],
            unit_send.at[route, by], unit_recv.at[route, by], on_route(route, target),
        )

    def start_grad(by, carry):
        for route in range(2):
            code(route, shifted(mine[route], by, shots))
            grad_copy(route, by).start()
            unit_copy(route, by).start()
        return carry

    lax.fori_loop(1, shots, start_grad, 0)
    for route in range(2):
        code(route, mine[route])
        grads_all[route, mine[route]] = grads_ref[route, mine[route]]
        units_all[route, mine[route]] = units_ref[route, mine[route]]

    def spread(route, by):
        sender = shifted(mine[route], shots - by, shots)
        for field in range(2):
            unit = units_all[route, sender, field : field + 1]
            for pair in range(APX // 2):
                values = grads_all[route, sender, field, pair].astype(F32) * unit
                turned = [turn(values[8 * i : 8 * i + 8], lane_block) for i in range(2)]
                high, low = split_two(jnp.concatenate(turned, axis=0))
                rows = pl.ds(pl.multiple_of(sender * positions + pair * 16, 16), 16)
                spread_ref[route, 0, rows, field * NZ : field * NZ + NZ] = high
                spread_ref[route, 1, rows, field * NZ : field * NZ + NZ] = low

    def returned(by, carry):
        for route in range(2):
            grad_copy(route, by).wait_recv()
            unit_copy(route, by).wait_recv()
            spread(route, by)
        return carry

    for route in range(2):
        spread(route, 0)
    lax.fori_loop(1, shots, returned, 0)

    block = depths * owned
    parts = [spread_ref[route].reshape(2 * shots * positions, 2 * NZ) for route in range(2)]

    def gx_copy(route, along):
        target = shifted(x, along, across)
        return remote(
            whole_levels.at[route, rows_at(target * block, block)], from_x.at[route, along],
            gx_send.at[route, along], gx_recv.at[route, along], (mine[0], target * depths + z),
        )

    def gx_lines(route, along):
        target = shifted(x, along, across)
        return remote(
            whole_lines.at[route, target], lines_x.at[route, along],
            xu_send.at[route, along], xu_recv.at[route, along], (mine[0], target * depths + z),
        )

    def merge(route, along):
        target = shifted(x, along, across)
        rows = rows_at(target * block, block)
        added = jnp.dot(place_ref[route, rows], parts[route], preferred_element_type=F32)
        if along == 0:
            column[route] = added
            return
        coded, units = row_levels(added)
        whole_levels[route, rows] = coded
        whole_lines[route, target] = units
        gx_copy(route, along).start()
        gx_lines(route, along).start()

    for route in range(2):
        for along in (2, 1, 3):
            merge(route, along)
    for route in range(2):
        merge(route, 0)

    def sum_x(route):
        summed = column[route]
        for along in (1, 3, 2):
            gx_copy(route, along).wait_recv()
            gx_lines(route, along).wait_recv()
            summed = summed + from_levels(from_x[route, along], jnp.transpose(lines_x[route, along]))
        column[route] = summed

    home = lax.rem(3 * y + z, depths)

    def gz_copy(by):
        target = shifted(z, by, depths)
        return remote(
            column.at[0, rows_at(target * owned, owned)], from_z.at[0, by],
            gz_send.at[0, by], gz_recv.at[0, by], (mine[0], x * depths + target),
        )

    def gy_copy(by):
        target = shifted(z, by, depths)
        return remote(
            column.at[1, rows_at(target * owned, owned)], from_z.at[1, y],
            gz_send.at[1, by], gz_recv.at[1, y], (home * 2 + core, x * depths + target),
        )

    def gy_arrival(from_y):
        return remote(
            column.at[1, rows_at(z * owned, owned)], from_z.at[1, from_y],
            gz_send.at[1, 0], gz_recv.at[1, from_y], (home * 2 + core, x * depths + shifted(z, 1, depths)),
        )

    def start_gz(by, carry):
        gz_copy(by).start()
        return carry

    def start_gy(by, carry):
        gy_copy(by).start()
        return carry

    sum_x(0)
    lax.fori_loop(1, depths, start_gz, 0)
    sum_x(1)
    lax.fori_loop(1, depths, start_gy, 0)

    @pl.when(home != y)
    def _():
        gy_copy(0).start()

    from_z[0, 0] = column[0, rows_at(z * owned, owned)]

    @pl.when(home == y)
    def _():
        from_z[1, y] = column[1, rows_at(z * owned, owned)]

    def end_z(by, carry):
        gz_copy(by).wait_recv()
        return carry

    def end_y(from_y, carry):
        @pl.when(jnp.logical_or(from_y != y, home != y))
        def _():
            gy_arrival(from_y).wait_recv()

        return carry

    lax.fori_loop(1, depths, end_z, 0)
    lax.fori_loop(0, depths, end_y, 0)
    for route in range(2):
        ended = from_z[route, 0]
        for by in range(1, depths):
            ended = ended + from_z[route, by]
        for field in range(2):
            lanes = (2 * field + route) * NZ
            out_ref[:, lanes : lanes + NZ] = ended[:, field * NZ : field * NZ + NZ]

    def finish_shots(by, carry):
        for route in range(2):
            shot_copy(route, by).wait_send()
            name_copy(route, by).wait_send()
            grad_copy(route, by).wait_send()
            unit_copy(route, by).wait_send()
        return carry

    def finish_z(by, carry):
        z_copy(by).wait_send()
        gz_copy(by).wait_send()
        gy_copy(by).wait_send()
        return carry

    lax.fori_loop(1, shots, finish_shots, 0)
    lax.fori_loop(1, depths, finish_z, 0)
    for route in range(2):
        for along in range(1, across):
            x_copy(route, along).wait_send()
            gx_copy(route, along).wait_send()
            gx_lines(route, along).wait_send()

    @pl.when(home != y)
    def _():
        gy_copy(0).wait_send()


def shot_gradients(tile_store, aperture, model, source, pulses, cells, traces, fwd, adj, shots, tiles):
    vmem = pl.BlockSpec(memory_space=pltpu.VMEM)
    smem = pl.BlockSpec(memory_space=pltpu.SMEM)
    hbm = pl.BlockSpec(memory_space=pltpu.HBM)
    owned = model.shape[0]
    lanes = model.shape[1] // shots
    depths = DEPTH_CHIPS
    across = tiles // depths
    total = tiles * owned
    positions = APX * APZ
    groups = shots * positions // NZ
    rows = depths * owned
    volume = (NX, NY, NZ)
    padded = (NX + 8, NY, NZ)
    int16 = jnp.int16
    dma = pltpu.SemaphoreType.DMA
    depth, middle = depth_matrix(), middle_matrix()
    return pl.pallas_call(
        shot_kernel,
        out_shape=jax.ShapeDtypeStruct((owned, lanes), F32),
        in_specs=[vmem, vmem, vmem, smem, smem, vmem, vmem, hbm, hbm, hbm, hbm],
        out_specs=vmem,
        scratch_shapes=[
            pltpu.VMEM(depth.shape, BF16),
            pltpu.VMEM(middle.shape, BF16),
            pltpu.VMEM(depth.shape, F32),
            pltpu.VMEM(middle.shape, F32),
            dma((6,)),
            pltpu.VMEM((depths, 2, owned, 2 * NZ), BF16),
            pltpu.VMEM((8, NZ), F32),
            pltpu.VMEM((tiles, 2, owned, 2 * NZ), BF16),
            pltpu.VMEM((2, shots * positions, total), BF16),
            pltpu.VMEM((2, shots, 8, NZ), F32),
            pltpu.VMEM((2, shots, positions, 2 * NZ), BF16),
            pltpu.VMEM((2, shots, positions, 2 * NZ), BF16),
            pltpu.VMEM(padded, F32),
            pltpu.VMEM(volume, F32),
            pltpu.VMEM((3,) + volume, F32),
            pltpu.VMEM((2,) + padded, F32),
            pltpu.VMEM((2,) + padded, F32),
            pltpu.VMEM((STEPS,) + volume, F32),
            pltpu.VMEM((STEPS, 3) + volume, F32),
            pltpu.VMEM((STEPS,) + volume, F32),
            pltpu.VMEM((NX * NY, NREC), BF16),
            pltpu.VMEM(volume, F32),
            pltpu.VMEM((2,) + volume, F32),
            pltpu.VMEM((2, B, 2, APX // 2, 16, NZ), int16),
            pltpu.VMEM((2, B, 2, NZ), F32),
            pltpu.VMEM((2, shots, 2, APX // 2, 16, NZ), int16),
            pltpu.VMEM((2, shots, 2, NZ), F32),
            pltpu.VMEM((2, total, 2 * groups * NZ), BF16),
            pltpu.VMEM((2, 2, shots * positions, 2 * NZ), BF16),
            pltpu.VMEM((2, total, 2 * NZ), int16),
            pltpu.VMEM((2, across, 8, rows), F32),
            pltpu.VMEM((2, across, rows, 2 * NZ), int16),
            pltpu.VMEM((2, across, 8, rows), F32),
            pltpu.VMEM((2, rows, 2 * NZ), F32),
            pltpu.VMEM((2, depths, owned, 2 * NZ), F32),
            dma((depths,)), dma((depths,)),
            dma((2, across)), dma((2, across)),
            dma((2, shots)), dma((2, shots)), dma((2, shots)), dma((2, shots)),
            dma((2, shots)), dma((2, shots)), dma((2, shots)), dma((2, shots)),
            dma((2, across)), dma((2, across)), dma((2, across)), dma((2, across)),
            dma((2, depths)), dma((2, depths)),
        ],
        compiler_params=pltpu.CompilerParams(
            collective_id=0, has_side_effects=True, vmem_limit_bytes=56 * 1024 * 1024
        ),
        cost_estimate=pl.CostEstimate(flops=2 * 10**9, bytes_accessed=5 * 2**20, transcendentals=0),
        name="shot_gradients",
    )(
        tile_store, aperture, model, source, pulses, cells, traces, fwd, adj,
        jnp.asarray(depth.astype(np.float32)), jnp.asarray(middle.astype(np.float32)),
    )


def per_device(
    tile_store, apertures, model, fwd_states, adj_states, source_cell, wavelet, receiver_cells, residuals
):
    shots, tiles = lax.axis_size("shot"), lax.axis_size("tile")
    owned = model.shape[0]
    sums = shot_gradients(
        tile_store.reshape(1, -1), apertures, model.reshape(owned, -1), source_cell, wavelet,
        receiver_cells, residuals[0], fwd_states, adj_states, shots, tiles,
    )
    return sums.reshape(owned, 2, -1)


def solution(mesh):
    return jax.shard_map(
        per_device,
        mesh=mesh,
        in_specs=(
            P(),
            P(("shot", "tile"), None),
            P("tile", None, None),
            P(("shot", "tile"), None, None, None, None),
            P(("shot", "tile"), None, None, None, None),
            P(("shot", "tile")),
            P(("shot", "tile"), None),
            P(("shot", "tile"), None),
            P(("shot", "tile"), None, None),
        ),
        out_specs=P("tile", None, "shot"),
        check_vma=False,
    )
```

time: 105 us -> 99.2 us (0.945)
  the two profiles are of different devices: /device:TPU:1 before, /device:TPU:6 now
where the time goes in v4:
time: 99.2 us; the launch traced here: 98.9 us
  Pallas kernels  95.1 us (96%)
  local copies, waits for them, and re-layouts  3.19 us (3%)
    pallas_call x1, Pallas kernels, shot_gradients(): pl.pallas_call(shot_kernel, out_shape=jax.ShapeDtypeStruct((owned, lanes)...  95.1 us

profile of v4, /device:TPU:6, one launch (start us, length us, event | category | flops | bytes accessed | tf_op | source)
XLA Modules:
  0.0 98.9 jit_solution(3802892325885053939)
XLA Ops:
  0.7 1.8 %copy.12 = bf16[2,8,2,4096]{3,1,2,0:T(8,128)(2,1)} copy(bf16[2,8,2,4096]{3,2,1,0:T(2,128)(2,1)} %bitcast.4) | data formatting | bytes 524288
  2.4 95.1 %shot_gradients.1 = f32[16,512]{1,0:T(8,128)} custom-call(s32[1,512]{1,0:T(1,128)} %bitcast.7, s32[1,32]{1,0:T(1,128)} %aperture_ref.1, bf16[16,8192]{1,0:T(8,128)(2,1)} %bitcast.5, s32[1]{0:T(128)S(6)} %copy.13.source_ref, f32[1,8]{1,0:T(1,128)} %pulse_ref.1, s32[1,256]{1,0:T(1,128)} %cells_ref.1, f32[8,256]{1,0:T(8,128)} %bitcast.6, ...), custom_call_target="tpu_custom_call" | custom-call | flops 2000000000 | bytes 5242880 | tf_op jit(solution)/shard_map/shot_gradients/pallas_call | solution.py:737
  97.6 1.4 %reshape.11 = f32[16,2,256]{2,1,0:T(2,128)} reshape(f32[16,512]{1,0:T(8,128)} %shot_gradients.1) | data formatting | bytes 65536 | tf_op jit(solution)/shard_map/reshape | solution.py:805

commit v5 on v4

--- a/solution.py
+++ b/solution.py
@@ -122,6 +122,10 @@
 
 def shifted(index, by, size):
     return lax.rem(index + by, size)
+
+
+def near_first(i, size):
+    return jnp.where(lax.rem(i, 2) == 1, lax.div(i + 1, 2), size - lax.div(i, 2))
 
 
 def chunk_of(route, index, y):
@@ -364,8 +368,8 @@
         picked = jnp.dot(pick_ref[route], held, preferred_element_type=F32)
         outgoing[route] = picked.astype(BF16).reshape(shots, positions, 2 * NZ)
 
-        def start_shot(by, carry):
-            shot_copy(route, by).start()
+        def start_shot(i, carry):
+            shot_copy(route, near_first(shots - i, shots)).start()
             return carry
 
         lax.fori_loop(1, shots, start_shot, 0)
@@ -429,7 +433,8 @@
                 else:
                     gain_ref[at + 4, 8 * route : 8 * route + 8] = turned
 
-    def arrived(by, carry):
+    def arrived(i, carry):
+        by = near_first(i, shots)
         for route in range(2):
             shot_copy(route, by).wait_recv()
             unpack(route, by)
@@ -544,7 +549,8 @@
             unit_send.at[route, by], unit_recv.at[route, by], on_route(route, target),
         )
 
-    def start_grad(by, carry):
+    def start_grad(i, carry):
+        by = near_first(shots - i, shots)
         for route in range(2):
             code(route, shifted(mine[route], by, shots))
             grad_copy(route, by).start()
@@ -569,19 +575,7 @@
                 spread_ref[route, 0, rows, field * NZ : field * NZ + NZ] = high
                 spread_ref[route, 1, rows, field * NZ : field * NZ + NZ] = low
 
-    def returned(by, carry):
-        for route in range(2):
-            grad_copy(route, by).wait_recv()
-            unit_copy(route, by).wait_recv()
-            spread(route, by)
-        return carry
-
-    for route in range(2):
-        spread(route, 0)
-    lax.fori_loop(1, shots, returned, 0)
-
     block = depths * owned
-    parts = [spread_ref[route].reshape(2 * shots * positions, 2 * NZ) for route in range(2)]
 
     def gx_copy(route, along):
         target = shifted(x, along, across)
@@ -600,7 +594,8 @@
     def merge(route, along):
         target = shifted(x, along, across)
         rows = rows_at(target * block, block)
-        added = jnp.dot(place_ref[route, rows], parts[route], preferred_element_type=F32)
+        parts = spread_ref[route].reshape(2 * shots * positions, 2 * NZ)
+        added = jnp.dot(place_ref[route, rows], parts, preferred_element_type=F32)
         if along == 0:
             column[route] = added
             return
@@ -611,6 +606,17 @@
         gx_lines(route, along).start()
 
     for route in range(2):
+        spread(route, 0)
+    for route in range(2):
+
+        def returned(i, carry):
+            by = near_first(i, shots)
+            grad_copy(route, by).wait_recv()
+            unit_copy(route, by).wait_recv()
+            spread(route, by)
+            return carry
+
+        lax.fori_loop(1, shots, returned, 0)
         for along in (2, 1, 3):
             merge(route, along)
     for route in range(2):

time: 99.2 us -> 96.5 us (0.973)
  the two profiles are of different devices: /device:TPU:6 before, /device:TPU:8 now
where the time goes in v5:
time: 96.5 us; the launch traced here: 96.3 us
  Pallas kernels  92.4 us (96%)
  local copies, waits for them, and re-layouts  3.19 us (3%)
    pallas_call x1, Pallas kernels, shot_gradients(): pl.pallas_call(shot_kernel, out_shape=jax.ShapeDtypeStruct((owned, lanes)...  92.4 us

profile of v5, /device:TPU:8, one launch (start us, length us, event | category | flops | bytes accessed | tf_op | source)
XLA Modules:
  0.0 96.3 jit_solution(1137231572104788239)
XLA Ops:
  0.7 1.8 %copy.12 = bf16[2,8,2,4096]{3,1,2,0:T(8,128)(2,1)} copy(bf16[2,8,2,4096]{3,2,1,0:T(2,128)(2,1)} %bitcast.4) | data formatting | bytes 524288
  2.4 92.4 %shot_gradients.1 = f32[16,512]{1,0:T(8,128)} custom-call(s32[1,512]{1,0:T(1,128)} %bitcast.7, s32[1,32]{1,0:T(1,128)} %aperture_ref.1, bf16[16,8192]{1,0:T(8,128)(2,1)} %bitcast.5, s32[1]{0:T(128)S(6)} %copy.13.source_ref, f32[1,8]{1,0:T(1,128)} %pulse_ref.1, s32[1,256]{1,0:T(1,128)} %cells_ref.1, f32[8,256]{1,0:T(8,128)} %bitcast.6, ...), custom_call_target="tpu_custom_call" | custom-call | flops 2000000000 | bytes 5242880 | tf_op jit(solution)/shard_map/shot_gradients/pallas_call | solution.py:743
  94.9 1.4 %reshape.11 = f32[16,2,256]{2,1,0:T(2,128)} reshape(f32[16,512]{1,0:T(8,128)} %shot_gradients.1) | data formatting | bytes 65536 | tf_op jit(solution)/shard_map/reshape | solution.py:811

commit v6 on v5

--- a/solution.py
+++ b/solution.py
@@ -693,8 +693,7 @@
         for by in range(1, depths):
             ended = ended + from_z[route, by]
         for field in range(2):
-            lanes = (2 * field + route) * NZ
-            out_ref[:, lanes : lanes + NZ] = ended[:, field * NZ : field * NZ + NZ]
+            out_ref[:, field, route * NZ : route * NZ + NZ] = ended[:, field * NZ : field * NZ + NZ]
 
     def finish_shots(by, carry):
         for route in range(2):
@@ -742,7 +741,7 @@
     depth, middle = depth_matrix(), middle_matrix()
     return pl.pallas_call(
         shot_kernel,
-        out_shape=jax.ShapeDtypeStruct((owned, lanes), F32),
+        out_shape=jax.ShapeDtypeStruct((owned, 2, lanes // 2), F32),
         in_specs=[vmem, vmem, vmem, smem, smem, vmem, vmem, hbm, hbm, hbm, hbm],
         out_specs=vmem,
         scratch_shapes=[
@@ -804,11 +803,10 @@
 ):
     shots, tiles = lax.axis_size("shot"), lax.axis_size("tile")
     owned = model.shape[0]
-    sums = shot_gradients(
+    return shot_gradients(
         tile_store.reshape(1, -1), apertures, model.reshape(owned, -1), source_cell, wavelet,
         receiver_cells, residuals[0], fwd_states, adj_states, shots, tiles,
     )
-    return sums.reshape(owned, 2, -1)
 
 
 def solution(mesh):

time: 96.5 us -> 96.5 us (level)
    reshape x1 -> x0, local copies, waits for them, and re-layouts: 1.39 us -> none  [per_device(): return sums.reshape(owned, 2, -1)]
    unnamed x1 -> x2, local copies, waits for them, and re-layouts: 1.79 us -> 3.17 us
where the time goes in v6:
time: 96.5 us; the launch traced here: 96.3 us
  Pallas kernels  92.4 us (96%)
  local copies, waits for them, and re-layouts  3.17 us (3%)
    pallas_call x1, Pallas kernels, shot_gradients(): pl.pallas_call(shot_kernel, out_shape=jax.ShapeDtypeStruct((owned, 2, lan...  92.4 us
    unnamed x2, local copies, waits for them, and re-layouts  3.17 us

profile of v6, /device:TPU:8, one launch (start us, length us, event | category | flops | bytes accessed | tf_op | source)
XLA Modules:
  0.0 96.3 jit_solution(7746524364458071860)
XLA Ops:
  0.7 1.8 %copy.12 = bf16[2,8,2,4096]{3,1,2,0:T(8,128)(2,1)} copy(bf16[2,8,2,4096]{3,2,1,0:T(2,128)(2,1)} %bitcast.4) | data formatting | bytes 524288
  2.4 92.4 %shot_gradients.1 = f32[16,2,256]{2,1,0:T(2,128)} custom-call(s32[1,512]{1,0:T(1,128)} %bitcast.7, s32[1,32]{1,0:T(1,128)} %aperture_ref.1, bf16[16,8192]{1,0:T(8,128)(2,1)} %bitcast.5, s32[1]{0:T(128)S(6)} %copy.14.source_ref, f32[1,8]{1,0:T(1,128)} %pulse_ref.1, s32[1,256]{1,0:T(1,128)} %cells_ref.1, f32[8,256]{1,0:T(8,128)} %bitcast.6, ...), custom_call_target="tpu_custom_call" | custom-call | flops 2000000000 | bytes 5242880 | tf_op jit(solution)/shard_map/shot_gradients/pallas_call | solution.py:742
  94.9 1.4 %copy.15 = f32[16,2,256]{2,1,0:T(2,128)} copy(f32[16,2,256]{2,1,0:T(2,128)} %shot_gradients.1) | data formatting | bytes 65536
